TPU v7x, 32 devices: a whole 2x2x4 slice. The times are simulated.
32 devices in a mesh: dp: 8 (over y, x, core), mp: 4 (over z).
Axes of the slice: x: 2, y: 2, z: 4, core: 2. Of those that a mesh axis runs over, the one named last changes fastest.
Arguments:
- feats: bfloat16 [4096, 768], P(('dp', 'mp')), may hold values from -6 to 6
- edge_owner: int32 [65536, 1], P(('dp', 'mp')), may hold values from 0 to 31; in each aligned block of 2048 rows (0 to 2047, 2048 to 4095, ...) at most 128 rows name the same one
- edge_row: int32 [65536], P(('dp', 'mp')), may hold values from 0 to 2047
- counts: int32 [4096], P(('dp', 'mp')), may hold values from 12 to 16
- table: float32 [65536, 128], P(('dp', 'mp')), may hold values from -6 to 6
- moment1: float32 [65536, 128], P(('dp', 'mp')), may hold values from -3 to 3
- moment2: float32 [65536, 128], P(('dp', 'mp')), may hold values from 0.001 to 0.1
- w_self: bfloat16 [768, 1024], replicated, may hold values from -0.21875 to 0.21875
- w_rel: bfloat16 [128, 1024], replicated, may hold values from -0.5 to 0.5
- cotangent: float32 [4096, 1024], P(('dp', 'mp')), may hold values from -6 to 6
- next_owner: int32 [4096, 1], P(('dp', 'mp')), may hold values from 0 to 31; in each aligned block of 128 rows (0 to 127, 128 to 255, ...) at most 8 rows name the same one
- next_row: int32 [4096], P(('dp', 'mp')), may hold values from 0 to 1023
- paper_table: bfloat16 [32768, 768], P(('dp', 'mp')), may hold values from -6 to 6
Outputs:
- new_table: float32 [65536, 128], P(('dp', 'mp'))
- new_moment1: float32 [65536, 128], P(('dp', 'mp'))
- new_moment2: float32 [65536, 128], P(('dp', 'mp'))
- grad_self: float32 [768, 1024], replicated
- grad_rel: float32 [128, 1024], replicated
- next_feats: bfloat16 [4096, 768], P(('dp', 'mp'))
Inputs may be any that keep to these rules, and one draw needn't show every extreme that they name: `edge_owner`: in the author slots of one device at most 128 name one owner, a bound that some block reaches. `next_owner`: in the next seeds of one device at most 8 name one owner, a bound that some block reaches.
All inputs are finite; a program needn't handle non-finite values.
Results may differ from a plain program's by a relative error of at most 0.0049.
Values may be sent and summed in bfloat16 or wider, within the bound.
A program may use at most 64 MiB of HBM per device.

v0:
```python
import jax
import jax.numpy as jnp
from jax import lax
from jax.sharding import PartitionSpec as P


def place_slots(owner, capacity, count_dev):
    owner_col = owner[:, 0]
    onehot = (owner_col[:, None] == jnp.arange(count_dev, dtype=jnp.int32)[None, :]).astype(
        jnp.int32
    )
    before = jnp.cumsum(onehot, axis=0) - onehot
    slot = jnp.sum(before * onehot, axis=1)
    return owner_col * capacity + slot


def shards(
    feats,
    edge_owner,
    edge_row,
    counts,
    table,
    moment1,
    moment2,
    w_self,
    w_rel,
    cotangent,
    next_owner,
    next_row,
    paper_table,
):
    n_dp = lax.axis_size("dp")
    n_mp = lax.axis_size("mp")
    devs = n_dp * n_mp
    seeds = counts.shape[0]
    slots_per = edge_row.shape[0] // seeds
    emb = table.shape[1]
    width = paper_table.shape[1]
    capacity = max(2, 2 * edge_row.shape[0] // devs)
    fcapacity = max(2, 2 * seeds // devs)
    live = jnp.arange(slots_per, dtype=jnp.int32)[None, :] < counts[:, None]
    count_f = counts.astype(jnp.float32)
    where_to = place_slots(edge_owner, capacity, devs)
    asked = (
        jnp.full((devs * capacity,), -1, jnp.int32)
        .at[where_to]
        .set(jnp.where(live.reshape(-1), edge_row, -1))
    )
    wanted_part = lax.all_to_all(
        asked.reshape(devs, capacity), ("dp", "mp"), split_axis=0, concat_axis=0, tiled=True
    )
    wanted = wanted_part
    answer = lax.all_to_all(
        jnp.take(table, jnp.maximum(wanted_part, 0), axis=0),
        ("dp", "mp"),
        split_axis=0,
        concat_axis=0,
        tiled=True,
    )
    wanted = wanted.reshape(devs * capacity)
    fetched = answer.reshape(devs * capacity, emb)
    edge_vals = jnp.take(fetched, where_to, axis=0).reshape(seeds, slots_per, emb)
    agg = (
        jnp.sum(jnp.where(live[:, :, None], edge_vals, jnp.float32(0.0)), axis=1) / count_f[:, None]
    )
    agg_b = agg.astype(jnp.bfloat16)
    pre = jnp.dot(feats, w_self, preferred_element_type=jnp.float32) + jnp.dot(
        agg_b, w_rel, preferred_element_type=jnp.float32
    )
    sig = jax.nn.sigmoid(pre)
    dpre = (cotangent * sig * (1.0 + pre * (1.0 - sig))).astype(jnp.bfloat16)
    part_self = lax.dot_general(
        feats, dpre, (((0,), (0,)), ((), ())), preferred_element_type=jnp.float32
    )
    part_rel = lax.dot_general(
        agg_b, dpre, (((0,), (0,)), ((), ())), preferred_element_type=jnp.float32
    )
    dagg = lax.dot_general(
        dpre, w_rel, (((1,), (1,)), ((), ())), preferred_element_type=jnp.float32
    )
    slot_grad = jnp.where(
        live[:, :, None], (dagg / count_f[:, None])[:, None, :], jnp.float32(0.0)
    ).reshape(seeds * slots_per, emb)
    outgoing = jnp.zeros((devs * capacity, emb), jnp.float32).at[where_to].set(slot_grad)
    arrived = lax.all_to_all(
        outgoing.reshape(devs, capacity, emb).astype(jnp.bfloat16),
        ("dp", "mp"),
        split_axis=0,
        concat_axis=0,
        tiled=True,
    ).astype(jnp.float32)
    arrived = arrived.reshape(devs * capacity, emb)
    valid = wanted >= 0
    safe_rows = jnp.maximum(wanted, 0)
    row_grad = (
        jnp.zeros(table.shape, jnp.float32)
        .at[safe_rows]
        .add(jnp.where(valid[:, None], arrived, jnp.float32(0.0)))
    )
    hits = jnp.zeros((table.shape[0],), jnp.int32).at[safe_rows].add(valid.astype(jnp.int32))
    touched = (hits > 0)[:, None]
    m_new = 0.9 * moment1 + 0.1 * row_grad
    v_new = 0.999 * moment2 + 0.001 * row_grad * row_grad
    update = 0.05 * (m_new / (1.0 - 0.9**10)) / (jnp.sqrt(v_new / (1.0 - 0.999**10)) + 1e-08)
    new_table = jnp.where(touched, table - update, table)
    new_moment1 = jnp.where(touched, m_new, moment1)
    new_moment2 = jnp.where(touched, v_new, moment2)
    grad_self, grad_rel = lax.psum((part_self, part_rel), ("dp", "mp"))
    paper_place = place_slots(next_owner, fcapacity, devs)
    paper_asked = jnp.full((devs * fcapacity,), -1, jnp.int32).at[paper_place].set(next_row)
    paper_rows = lax.all_to_all(
        jnp.take(
            paper_table,
            jnp.maximum(
                lax.all_to_all(
                    paper_asked.reshape(devs, fcapacity),
                    ("dp", "mp"),
                    split_axis=0,
                    concat_axis=0,
                    tiled=True,
                ),
                0,
            ),
            axis=0,
        ),
        ("dp", "mp"),
        split_axis=0,
        concat_axis=0,
        tiled=True,
    )
    next_feats = jnp.take(paper_rows.reshape(devs * fcapacity, width), paper_place, axis=0)
    return (new_table, new_moment1, new_moment2, grad_self, grad_rel, next_feats)


def solution(mesh):
    in_specs = (
        P(("dp", "mp"), None),
        P(("dp", "mp"), None),
        P(("dp", "mp")),
        P(("dp", "mp")),
        P(("dp", "mp"), None),
        P(("dp", "mp"), None),
        P(("dp", "mp"), None),
        P(),
        P(),
        P(("dp", "mp"), None),
        P(("dp", "mp"), None),
        P(("dp", "mp")),
        P(("dp", "mp"), None),
    )
    out_specs = (
        P(("dp", "mp"), None),
        P(("dp", "mp"), None),
        P(("dp", "mp"), None),
        P(),
        P(),
        P(("dp", "mp"), None),
    )
    return jax.shard_map(shards, mesh=mesh, in_specs=in_specs, out_specs=out_specs, check_vma=False)
```

profile of v0, /device:TPU:0, one launch (start us, length us, event | category | flops | bytes accessed | tf_op | source)
XLA Modules:
  0.0 347.9 jit_solution(1292934457891076019)
XLA Ops:
  7.2 0.9 fusion.12
  8.1 9.1 %reduce-window.6 = s32[32,16,128]{2,1,0:T(8,128)S(1)} reduce-window(s32[32,16,128]{2,1,0:T(8,128)S(1)} %fusion.12, s32[]{:T(128)} %constant.45.clone.1), window={size=1x1x128 pad=0_0x0_0x127_0}, to_apply=%region_0.0 | reduce-window | flops 8323072 | bytes 524292 | tf_op jit(solution)/shard_map/reduce-window
  18.3 8.6 %scatter_custom_fusion = s32[4096]{0:T(1024)} fusion(s32[2048]{0:T(1024)S(1)} %bitcast.84, s32[2048]{0:T(1024)S(1)} %broadcast_select_fusion.2, s32[]{:T(128)} %constant.52.clone.1), kind=kCustom, calls=%fused_computation.50 | custom fusion | bytes 16388 | tf_op jit(solution)/shard_map/scatter | solution.py:47
  26.9 7.3 %all-to-all-start = ((s32[32,1,128]{2,1,0:T(1,128)}), s32[32,1,128]{2,1,0:T(1,128)S(1)}, u32[]{:S(2)}, u32[]{:S(2)}) async-start(s32[32,1,128]{2,1,0:T(1,128)} %bitcast.7), calls=%async_computation | async-start | bytes 32768 | tf_op jit(solution)/shard_map/all_to_all | solution.py:49
  35.2 1.1 scatter_custom_fusion.4
  37.0 4.3 %all-to-all-done = s32[32,1,128]{2,1,0:T(1,128)S(1)} async-done(((s32[32,1,128]{2,1,0:T(1,128)}), s32[32,1,128]{2,1,0:T(1,128)S(1)}, u32[]{:S(2)}, u32[]{:S(2)}) %all-to-all-start) | async-done | bytes 16416 | tf_op jit(solution)/shard_map/all_to_all | solution.py:49
  41.3 2.5 all-to-all-start.3
  44.5 14.2 %gather_fusion = f32[4096,128]{1,0:T(8,128)} fusion(f32[2048,128]{1,0:T(8,128)S(1)} %copy-done.1, s32[4096]{0:T(1024)S(1)} %broadcast_clamp_fusion), kind=kCustom, calls=%fused_computation | custom fusion | bytes 4210688 | tf_op jit(solution)/shard_map/jit(_take)/gather | solution.py:54
  58.7 2.9 broadcast_select_fusion
  61.6 6.0 %all-to-all-start.1 = ((f32[32,128,128]{2,1,0:T(8,128)}), f32[32,128,128]{2,1,0:T(8,128)}, u32[]{:S(2)}, u32[]{:S(2)}) async-start(f32[32,128,128]{2,1,0:T(8,128)} %broadcast_select_fusion), calls=%async_computation.1 | async-start | bytes 4194304 | tf_op jit(solution)/shard_map/all_to_all | solution.py:53
  68.3 2.6 fusion.22
  71.2 1.2 gather_fusion.2
  72.4 0.9 bitcast_select_fusion.1
  73.3 41.8 %all-to-all-done.1 = f32[32,128,128]{2,1,0:T(8,128)} async-done(((f32[32,128,128]{2,1,0:T(8,128)}), f32[32,128,128]{2,1,0:T(8,128)}, u32[]{:S(2)}, u32[]{:S(2)}) %all-to-all-start.1) | async-done | bytes 2097184 | tf_op jit(solution)/shard_map/all_to_all | solution.py:53
  115.1 4.1 %all-to-all-start.4 = ((bf16[32,8,768]{2,1,0:T(8,128)(2,1)}), bf16[32,8,768]{2,1,0:T(8,128)(2,1)S(1)}, u32[]{:S(2)}, u32[]{:S(2)}) async-start(bf16[32,8,768]{2,1,0:T(8,128)(2,1)} %bitcast_select_fusion.1), calls=%async_computation.4 | async-start | bytes 786432 | tf_op jit(solution)/shard_map/all_to_all | solution.py:111
  119.2 9.2 %gather_fusion.1 = f32[2048,128]{1,0:T(8,128)} fusion(f32[4096,128]{1,0:T(8,128)} %bitcast.14, s32[2048]{0:T(1024)S(1)} %broadcast_clamp_fusion.1), kind=kCustom, calls=%fused_computation.1 | custom fusion | bytes 2105344 | tf_op jit(solution)/shard_map/jit(_take)/gather | solution.py:62
  128.5 2.7 select_reduce_fusion
  131.1 1.7 multiply_convert_fusion
  133.1 1.3 bitcast_select_fusion
  134.4 7.4 %scatter_custom_fusion.2 = f32[4096,128]{1,0:T(8,128)} fusion(s32[2048]{0:T(1024)} %bitcast.86, f32[2048,128]{1,0:T(8,128)} %bitcast_select_fusion, f32[]{:T(128)} %constant.57.clone.1), kind=kCustom, calls=%fused_computation.22 | custom fusion | bytes 2097664 | tf_op jit(solution)/shard_map/scatter | solution.py:84
  141.8 2.7 convert_element_type.35
  144.4 2.3 convolution_bitcast_fusion
  146.7 6.0 %all-to-all-start.2 = ((bf16[32,128,128]{2,1,0:T(8,128)(2,1)}), bf16[32,128,128]{2,1,0:T(8,128)(2,1)}, u32[]{:S(2)}, u32[]{:S(2)}) async-start(bf16[32,128,128]{2,1,0:T(8,128)(2,1)} %bitcast.74), calls=%async_computation.2 | async-start | bytes 2097152 | tf_op jit(solution)/shard_map/all_to_all | solution.py:85
  152.7 1.1 fusion.20
  153.9 23.0 %scatter_custom_fusion.1 = s32[2048]{0:T(1024)S(1)} fusion(s32[4096]{0:T(1024)S(1)} %maximum_bitcast_fusion, s32[4096]{0:T(1024)} %get-tuple-element.34, s32[]{:T(128)} %constant.45.clone.1), kind=kCustom, calls=%fused_computation.57 | custom fusion | flops 4096 | bytes 8704 | tf_op jit(solution)/shard_map/scatter-add | solution.py:100
  176.9 0.9 gather_fusion.3
  177.8 0.8 broadcast_select_fusion.1
  178.6 128.4 %all-reduce.3.cloned.1.call-done = (f32[768,1024]{0,1:T(8,128)}, f32[128,1024]{1,0:T(8,128)}) async-done(((f32[768,1024]{0,1:T(8,128)}, f32[128,1024]{1,0:T(8,128)}), (f32[768,1024]{0,1:T(8,128)}, f32[128,1024]{1,0:T(8,128)})) %all-reduce.3.cloned.1.call-update) | async-done | bytes 3670032 | tf_op jit(solution)/shard_map/psum | solution.py:108
  307.0 3.5 %copy.35 = f32[768,1024]{1,0:T(8,128)} copy(f32[768,1024]{0,1:T(8,128)} %get-tuple-element.30) | data formatting | bytes 6291456
  310.5 26.3 %scatter_custom_fusion.3 = f32[2048,128]{1,0:T(8,128)} fusion(s32[4096]{0:T(1024)S(1)} %maximum_bitcast_fusion, bf16[4096,128]{1,0:T(8,128)(2,1)} %bitcast.28, f32[]{:T(128)} %constant.57.clone.1, pred[4096]{0:T(1024)(128)(4,1)S(1)} %copy-done.8), kind=kCustom, calls=%fused_computation.10 | custom fusion | flops 1572864 | bytes 2102272 | tf_op jit(solution)/shard_map/scatter-add | solution.py:98
  336.8 3.5 %fusion.7 = (f32[2048,128]{1,0:T(8,128)}, f32[2048,128]{1,0:T(8,128)}, f32[2048,128]{1,0:T(8,128)}) fusion(f32[2048,128]{1,0:T(8,128)} %param.19, f32[2048,128]{1,0:T(8,128)} %scatter_custom_fusion.3, pred[2048]{0:T(1024)(128)(4,1)S(1)} %broadcast_compare_fusion, f32[2048,128]{1,0:T(8,128)S(1)} %copy-done.1, f32[2048,128]{1,0:T(8,128)} %param.18), kind=kLoop, calls=%fused_computation.26 | loop fusion | flops 3932160 | bytes 7342080 | tf_op jit(solution)/shard_map/jit(_where)/select_n | solution.py:107
  340.3 0.8 copy.41
  (71 shorter events, 4.7 us)
Async XLA Ops:
  7.2 64.1 %copy-start = (bf16[1024,768]{1,0:T(8,128)(2,1)S(1)}, bf16[1024,768]{1,0:T(8,128)(2,1)}, u32[]{:S(2)}) copy-start(bf16[1024,768]{1,0:T(8,128)(2,1)} %param.25) | copy-start | bytes 4718596
  7.2 10.7 %copy-start.4 = (s32[2048,1]{0,1:T(1,128)S(1)}, s32[2048,1]{0,1:T(1,128)}, u32[]{:S(2)}) copy-start(s32[2048,1]{0,1:T(1,128)} %param.14) | copy-start | bytes 24580
  7.2 10.9 %copy-start.16 = (s32[128]{0:T(128)S(1)}, s32[128]{0:T(128)}, u32[]{:S(2)}) copy-start(s32[128]{0:T(128)} %param.16) | copy-start | bytes 1540
  7.2 11.1 %copy-start.9 = (s32[2048]{0:T(1024)S(1)}, s32[2048]{0:T(1024)}, u32[]{:S(2)}) copy-start(s32[2048]{0:T(1024)} %param.15) | copy-start | bytes 24580
  7.2 27.0 %copy-start.10 = (s32[128,1]{0,1:T(1,128)S(1)}, s32[128,1]{0,1:T(1,128)}, u32[]{:S(2)}) copy-start(s32[128,1]{0,1:T(1,128)} %param.23) | copy-start | bytes 1540
  7.2 37.3 %copy-start.1 = (f32[2048,128]{1,0:T(8,128)S(1)}, f32[2048,128]{1,0:T(8,128)}, u32[]{:S(2)}) copy-start(f32[2048,128]{1,0:T(8,128)} %param.17) | copy-start | bytes 3145732
  18.1 50.2 %copy-start.5 = (s32[2048,1]{0,1:T(1,128)}, s32[2048,1]{0,1:T(1,128)S(1)}, u32[]{:S(2)}) copy-start(s32[2048,1]{0,1:T(1,128)S(1)} %get-tuple-element.37) | copy-start | bytes 24580
  18.3 16.0 %copy-start.6 = (pred[2048]{0:T(1024)(128)(4,1)}, pred[2048]{0:T(1024)(128)(4,1)S(1)}, u32[]{:S(2)}) copy-start(pred[2048]{0:T(1024)(128)(4,1)S(1)} %lt.58) | copy-start | bytes 6148
  26.9 14.4 %all-to-all-start = ((s32[32,1,128]{2,1,0:T(1,128)}), s32[32,1,128]{2,1,0:T(1,128)S(1)}, u32[]{:S(2)}, u32[]{:S(2)}) async-start(s32[32,1,128]{2,1,0:T(1,128)} %bitcast.7), calls=%async_computation | async-start | bytes 32768 | tf_op jit(solution)/shard_map/all_to_all | solution.py:49
  35.2 23.5 %copy-start.12 = (s32[128,1]{0,1:T(1,128)}, s32[128,1]{0,1:T(1,128)S(1)}, u32[]{:S(2)}) copy-start(s32[128,1]{0,1:T(1,128)S(1)} %get-tuple-element.33) | copy-start | bytes 1540
  41.3 20.3 %all-to-all-start.3 = ((s32[32,1,8]{2,1,0:T(1,128)}), s32[32,1,8]{2,1,0:T(1,128)S(1)}, u32[]{:S(2)}, u32[]{:S(2)}) async-start(s32[32,1,8]{2,1,0:T(1,128)} %bitcast.24), calls=%async_computation.3 | async-start | bytes 32768 | tf_op jit(solution)/shard_map/all_to_all | solution.py:115
  61.6 6.7 %copy-start.2 = (bf16[128,768]{1,0:T(8,128)(2,1)S(1)}, bf16[128,768]{1,0:T(8,128)(2,1)}, u32[]{:S(2)}) copy-start(bf16[128,768]{1,0:T(8,128)(2,1)} %param.13) | copy-start | bytes 589828
  61.6 53.5 %all-to-all-start.1 = ((f32[32,128,128]{2,1,0:T(8,128)}), f32[32,128,128]{2,1,0:T(8,128)}, u32[]{:S(2)}, u32[]{:S(2)}) async-start(f32[32,128,128]{2,1,0:T(8,128)} %broadcast_select_fusion), calls=%async_computation.1 | async-start | bytes 4194304 | tf_op jit(solution)/shard_map/all_to_all | solution.py:53
  115.1 31.6 %all-to-all-start.4 = ((bf16[32,8,768]{2,1,0:T(8,128)(2,1)}), bf16[32,8,768]{2,1,0:T(8,128)(2,1)S(1)}, u32[]{:S(2)}, u32[]{:S(2)}) async-start(bf16[32,8,768]{2,1,0:T(8,128)(2,1)} %bitcast_select_fusion.1), calls=%async_computation.4 | async-start | bytes 786432 | tf_op jit(solution)/shard_map/all_to_all | solution.py:111
  128.5 4.4 %copy-start.14 = (f32[128]{0:T(128)S(1)}, f32[128]{0:T(128)}, u32[]{:S(2)}) copy-start(f32[128]{0:T(128)} %convert_element_type.32) | copy-start | bytes 1540
  128.5 4.4 %copy-start.17 = (bf16[128,1024]{1,0:T(8,128)(2,1)S(1)}, bf16[128,1024]{1,0:T(8,128)(2,1)}, u32[]{:S(2)}) copy-start(bf16[128,1024]{1,0:T(8,128)(2,1)} %param.21) | copy-start | bytes 786436
  131.1 2.0 copy-start.7
  146.7 6.0 %copy-start.15 = (f32[128]{0:T(128)S(1)}, f32[128]{0:T(128)}, u32[]{:S(2)}) copy-start(f32[128]{0:T(128)} %convert_element_type.32) | copy-start | bytes 1540
  146.7 163.8 %all-to-all-start.2 = ((bf16[32,128,128]{2,1,0:T(8,128)(2,1)}), bf16[32,128,128]{2,1,0:T(8,128)(2,1)}, u32[]{:S(2)}, u32[]{:S(2)}) async-start(bf16[32,128,128]{2,1,0:T(8,128)(2,1)} %bitcast.74), calls=%async_computation.2 | async-start | bytes 2097152 | tf_op jit(solution)/shard_map/all_to_all | solution.py:85
  152.7 1.2 copy-start.13
  152.7 154.3 %all-reduce.3.cloned.1.call-start = ((), (), s32[]{:S(2)}) async-start(), calls=%async_computation.5 | async-start | bytes 7340032 | tf_op jit(solution)/shard_map/psum | solution.py:108
  153.9 23.9 %copy-start.11 = (pred[128]{0:T(512)(128)(4,1)S(1)}, pred[128]{0:T(512)(128)(4,1)}, u32[]{:S(2)}) copy-start(pred[128]{0:T(512)(128)(4,1)} %get-tuple-element.32) | copy-start | bytes 388
  307.0 3.5 %copy-start.8 = (pred[4096]{0:T(1024)(128)(4,1)S(1)}, pred[4096]{0:T(1024)(128)(4,1)}, u32[]{:S(2)}) copy-start(pred[4096]{0:T(1024)(128)(4,1)} %get-tuple-element.35) | copy-start | bytes 12292
  336.8 3.5 %copy-start.3 = (f32[128,1024]{1,0:T(8,128)S(1)}, f32[128,1024]{1,0:T(8,128)}, u32[]{:S(2)}) copy-start(f32[128,1024]{1,0:T(8,128)} %get-tuple-element.46) | copy-start | bytes 1572868
Sparse Core Ops, SparseCore 0:
  159.7 147.2 all-reduce.2
where the time goes:
time: 351 us; the launch traced here: 348 us
  waiting for transfers between devices  175 us (50%)
  other arithmetic  76.6 us (22%)
  local copies, waits for them, and re-layouts  48.5 us (14%)
  starting transfers between devices  25.9 us (7%)
  between operations  14.4 us (4%)
  matrix products  7.9 us (2%)
    psum x1, waiting for transfers between devices, shards(): grad_self, grad_rel = lax.psum((part_self, part_rel), ('dp', 'mp'))  128 us
    all_to_all x1, waiting for transfers between devices, shards(): lax.all_to_all(jnp.take(table, jnp.maximum(wanted_part, 0), axis=0), ('dp...  41.8 us
    scatter-add x1, other arithmetic, shards(): row_grad = jnp.zeros(table.shape, jnp.float32).at[safe_rows].add(jnp.wher...  26.3 us
    scatter-add x1, other arithmetic, shards(): jnp.zeros((table.shape[0],), jnp.int32).at[safe_rows]  23 us
    gather x1, local copies, waits for them, and re-layouts, shards(): jnp.take(table, jnp.maximum(wanted_part, 0), axis=0)  14.2 us
    another operation x3, other arithmetic  9.41 us
    gather x1, local copies, waits for them, and re-layouts, shards(): jnp.take(fetched, where_to, axis=0).reshape(seeds, slots_per, emb)  9.22 us
    scatter x1, local copies, waits for them, and re-layouts, shards(): asked = jnp.full((devs * capacity,), -1, jnp.int32).at[where_to].set(jnp....  8.62 us
  transfers between devices with their start and end apart: 6, of which 3 were waited for; matrix products, arithmetic and copies ran while one was open for 24% of the time, Pallas kernels for 0%

commit v1 on v0

v1 whole, which is shorter than its diff:
```python
import functools

import jax
import jax.numpy as jnp
from jax import lax
from jax.experimental import pallas as pl
from jax.experimental.pallas import tpu as pltpu
from jax.sharding import PartitionSpec as P

F32, BF16, I32 = jnp.float32, jnp.bfloat16, jnp.int32
LANES = 128
VMEM_LIMIT = 48 * 1024 * 1024
MESH = pl.DeviceIdType.MESH
VM = pl.BlockSpec(memory_space=pltpu.VMEM)


def dot_nt(a, b):
    return lax.dot_general(a, b, (((1,), (1,)), ((), ())), preferred_element_type=F32)


def dot_nn(a, b):
    return jnp.dot(a, b, preferred_element_type=F32)


def split(x):
    hi = x.astype(BF16)
    return hi, (x - hi.astype(F32)).astype(BF16)


def onehot(mask):
    return jnp.where(mask, 1.0, 0.0).astype(BF16)


def steps_of(n_dp, n_mp):
    return [(0, 1 << b) for b in range(n_dp.bit_length() - 1)] + [
        (1, 1 << b) for b in range(n_mp.bit_length() - 1)
    ]


def position_of(device, n_mp, steps):
    coords = (device // n_mp, device % n_mp)
    pos = 0
    for axis, w in steps:
        pos = pos * 2 + (coords[axis] // w) % 2
    return pos


def partners(steps):
    coords = (lax.axis_index("dp"), lax.axis_index("mp"))
    found = []
    for axis, w in steps:
        bit = lax.rem(coords[axis] // w, 2)
        other = coords[axis] + w * (1 - 2 * bit)
        found.append((bit, (other, coords[1]) if axis == 0 else (coords[0], other)))
    return found


def enter(found):
    barrier = pltpu.get_barrier_semaphore()
    for _, device in found:
        pl.semaphore_signal(barrier, inc=1, device_id=device, device_id_type=MESH)
    pl.semaphore_wait(barrier, len(found))


def rs_scratch(n, block, wires):
    shapes = []
    for s, wire in enumerate(wires):
        half = n >> (s + 1)
        shapes += [pltpu.VMEM((half, *block), wire), pltpu.VMEM((half, *block), F32)]
        shapes += [pltpu.VMEM((half, *block) if wire == BF16 else (1, 8, LANES), wire)]
    return shapes


def rs_start(cur, scratch, s, n, wire, bit, device, send, recv):
    half = n >> (s + 1)
    arrive, _, rounded = scratch[3 * s : 3 * s + 3]
    away = (1 - bit) * half
    if wire == BF16:

        @pl.loop(0, half)
        def _(i):
            rounded[i] = cur[away + i].astype(BF16)

        src = rounded
    else:
        src = cur.at[pl.ds(away, half)]
    copy = pltpu.make_async_remote_copy(
        src_ref=src, dst_ref=arrive, send_sem=send.at[s], recv_sem=recv.at[s],
        device_id=device, device_id_type=MESH,
    )
    copy.start()
    return copy


def rs_add(cur, scratch, s, n, bit):
    half = n >> (s + 1)
    arrive, total, _ = scratch[3 * s : 3 * s + 3]

    @pl.loop(0, half)
    def _(i):
        total[i] = cur[bit * half + i] + arrive[i].astype(F32)

    return total


def ag_start(out, s, n, pos, device, send, recv):
    size = n >> (s + 1)
    here = out.at[pl.ds((pos // size) * size, size)]
    copy = pltpu.make_async_remote_copy(
        src_ref=here, dst_ref=here, send_sem=send.at[s], recv_sem=recv.at[s],
        device_id=device, device_id_type=MESH,
    )
    copy.start()
    return copy


def my_position(found):
    pos = 0
    for bit, _ in found:
        pos = pos * 2 + bit
    return pos


def reduce_kernel(n, steps, wires, x, out, *rest):
    scratch, (send, recv) = rest[:-2], rest[-2:]
    found = partners(steps)
    enter(found)
    cur = x
    for s, (bit, device) in enumerate(found):
        rs_start(cur, scratch, s, n, wires[s], bit, device, send, recv).wait()
        cur = rs_add(cur, scratch, s, n, bit)
    out[...] = cur[0]


def exchange_kernel(n, steps, wires, grads, dagg, out_dagg, out_grads, *rest):
    scratch, (send, recv, gsend, grecv, hsend, hrecv) = rest[:-6], rest[-6:]
    found = partners(steps)
    pos = my_position(found)
    enter(found)
    out_dagg[pos] = dagg[...]
    cur = grads
    last = len(steps) - 1
    for s, (bit, device) in enumerate(found):
        first = rs_start(cur, scratch, s, n, wires[s], bit, device, send, recv)
        second = ag_start(out_dagg, last - s, n, pos, found[last - s][1], gsend, grecv)
        first.wait()
        cur = rs_add(cur, scratch, s, n, bit)
        second.wait()
    out_grads[pos] = cur[0].astype(BF16)
    for s in reversed(range(len(steps))):
        ag_start(out_grads, s, n, pos, found[s][1], hsend, hrecv).wait()


def place_kernel(n, cap, slots_per, owner, row, counts, out_row, out_seed):
    blocks = owner.shape[0]
    seeds = counts.shape[1]
    per = LANES // slots_per
    at_seed = lax.broadcasted_iota(I32, (blocks, seeds), 1)
    at_block = lax.broadcasted_iota(I32, (blocks, seeds), 0)
    spread = jnp.where(at_seed // per == at_block, counts[...].astype(F32), 0.0).astype(BF16)
    s_i = lax.broadcasted_iota(I32, (seeds, LANES), 0)
    l_i = lax.broadcasted_iota(I32, (seeds, LANES), 1)
    count = dot_nn(spread, onehot(lax.rem(s_i, per) == l_i // slots_per))
    lane = lax.broadcasted_iota(I32, (blocks, LANES), 1)
    live = lax.rem(lane, slots_per).astype(F32) < count - 0.5
    wanted = jnp.where(live, row[...] + 1, 0)
    seed = lax.broadcasted_iota(I32, (blocks, LANES), 0) * per + lane // slots_per
    parts = [(wanted // 64).astype(F32), lax.rem(wanted, 64).astype(F32), seed.astype(F32)]
    dev = lax.broadcasted_iota(I32, (n, LANES), 0)
    hot = [jnp.where(dev == owner[a : a + 1, :], 1.0, 0.0) for a in range(blocks)]
    t_i = lax.broadcasted_iota(I32, (LANES, LANES), 0)
    t_j = lax.broadcasted_iota(I32, (LANES, LANES), 1)
    before = dot_nn(jnp.concatenate([h.astype(BF16) for h in hot], axis=0), onehot(t_i < t_j))
    base = jnp.zeros((n, 1), F32)
    place = lax.broadcasted_iota(I32, (cap, LANES), 0).astype(F32)
    left, right = [], []
    for a in range(blocks):
        slot = jnp.sum(hot[a] * (before[a * n : (a + 1) * n] + base), axis=0, keepdims=True)
        base = base + jnp.sum(hot[a], axis=1, keepdims=True)
        right.append(onehot(place == slot))
        left.append(
            jnp.concatenate([(hot[a] * p[a : a + 1, :]).astype(BF16) for p in parts], axis=0)
        )
    got = dot_nt(jnp.concatenate(left, axis=1), jnp.concatenate(right, axis=1))
    out_row[...] = (got[:n] * 64.0 + got[n : 2 * n] - 1.0).astype(I32)
    out_seed[...] = got[2 * n :].astype(I32)


def seed_hot(seed, d, cap, seeds):
    q = LANES // cap
    lane = lax.broadcasted_iota(I32, (1, LANES), 1)
    which = seed[pl.ds(d, 1), :] + seeds * (lane // cap)
    return onehot(lax.broadcasted_iota(I32, (q * seeds, LANES), 0) == which)


def fetch_kernel(cap, places, rows, seed, table, out, packed):
    n_rows, emb = table.shape
    seeds = out.shape[2]
    q = LANES // cap
    flipped = table[...].T
    hi, lo = split(flipped)
    packed[:emb, :] = hi
    packed[emb:, :] = lo
    at = lax.broadcasted_iota(I32, (n_rows, LANES), 0)
    for d in range(0, rows.shape[0], 2):
        hot = jnp.concatenate([onehot(at == rows[d + j : d + j + 1, :]) for j in range(2)], axis=1)
        got = dot_nn(packed[...], hot)
        vals = got[:emb] + got[emb:]
        for j in range(2):
            v_hi, v_lo = split(vals[:, j * LANES : (j + 1) * LANES])
            both = dot_nt(jnp.concatenate([v_hi, v_lo], axis=0), seed_hot(seed, d + j, cap, seeds))
            sums = both[:emb] + both[emb:]
            for k in range(q):
                out[places[(d + j) * q + k]] = sums[:, k * seeds : (k + 1) * seeds]


def layer_kernel(agg_sum, counts, feats, w_self, w_rel, cot, out_parts, out_dagg):
    n, rows, _ = out_parts.shape
    width = w_self.shape[1]
    tiles = width // LANES
    count = counts[...].astype(F32)
    agg_t = agg_sum[...] / count
    agg_b = agg_t.T.astype(BF16)
    pre = dot_nn(feats[...], w_self[...]) + dot_nn(agg_b, w_rel[...])
    sig = 1.0 / (1.0 + jnp.exp(-pre))
    dpre = (cot[...] * sig * (1.0 + pre * (1.0 - sig))).astype(BF16)
    out_dagg[...] = (dot_nt(w_rel[...], dpre) / count).astype(BF16)
    flipped = [feats[...].astype(F32).T.astype(BF16), agg_t.astype(BF16)]
    pad = n // tiles * rows - flipped[0].shape[0] - flipped[1].shape[0]
    if pad:
        flipped.append(jnp.zeros((pad, agg_t.shape[1]), BF16))
    lhs = jnp.concatenate(flipped, axis=0)
    for i in range(n // tiles):
        got = dot_nn(lhs[i * rows : (i + 1) * rows], dpre)
        for t in range(tiles):
            out_parts[i * tiles + t] = got[:, t * LANES : (t + 1) * LANES]


def adam_kernel(cap, places, rows, seed, dagg, table, m1, m2, o_table, o_m1, o_m2, slot_g, hot):
    size, emb = table.shape
    seeds = dagg.shape[2]
    q = LANES // cap
    blocks = rows.shape[0]

    @pl.when(pl.program_id(0) == 0)
    def _():
        for d in range(blocks):
            grads = [dagg[places[d * q + k]] for k in range(q)]
            got = dot_nn(jnp.concatenate(grads, axis=1), seed_hot(seed, d, cap, seeds))
            slot_g[:emb, d * LANES : (d + 1) * LANES] = got.astype(BF16)
        slot_g[emb:, :] = jnp.ones((emb, blocks * LANES), BF16)

    at = lax.broadcasted_iota(I32, (size, LANES), 0) + pl.program_id(0) * size
    for d in range(blocks):
        hot[:, d * LANES : (d + 1) * LANES] = onehot(at == rows[d : d + 1, :])
    got = dot_nt(hot[...], slot_g[...])
    grad, touched = got[:, :emb], got[:, emb:] > 0.5
    m_new = 0.9 * m1[...] + 0.1 * grad
    v_new = 0.999 * m2[...] + 0.001 * grad * grad
    step = 0.05 * (m_new / (1.0 - 0.9**10)) / (jnp.sqrt(v_new / (1.0 - 0.999**10)) + 1e-08)
    o_table[...] = jnp.where(touched, table[...] - step, table[...])
    o_m1[...] = jnp.where(touched, m_new, m1[...])
    o_m2[...] = jnp.where(touched, v_new, m2[...])


def params(**more):
    return pltpu.CompilerParams(vmem_limit_bytes=VMEM_LIMIT, **more)


def place_slots(owner, capacity, count_dev):
    owner_col = owner[:, 0]
    hot = (owner_col[:, None] == jnp.arange(count_dev, dtype=I32)[None, :]).astype(I32)
    before = jnp.cumsum(hot, axis=0) - hot
    return owner_col * capacity + jnp.sum(before * hot, axis=1)


def all_to_all(x):
    return lax.all_to_all(x, ("dp", "mp"), split_axis=0, concat_axis=0, tiled=True)


def shards(
    feats,
    edge_owner,
    edge_row,
    counts,
    table,
    moment1,
    moment2,
    w_self,
    w_rel,
    cotangent,
    next_owner,
    next_row,
    paper_table,
):
    n_dp, n_mp = lax.axis_size("dp"), lax.axis_size("mp")
    n = n_dp * n_mp
    steps = steps_of(n_dp, n_mp)
    places = [position_of(d, n_mp, steps) for d in range(n)]
    seeds = counts.shape[0]
    edges = edge_row.shape[0]
    n_rows, emb = table.shape
    feat_w, hidden = w_self.shape
    width = paper_table.shape[1]
    cap = max(2, 2 * edges // n)
    fcap = max(2, 2 * seeds // n)
    blocks = n * cap // LANES
    counts_row = counts.reshape(1, seeds)

    asked_row, asked_seed = pl.pallas_call(
        functools.partial(place_kernel, n, cap, edges // seeds),
        out_shape=[jax.ShapeDtypeStruct((n, cap), I32)] * 2,
        in_specs=[VM] * 3,
        out_specs=[VM] * 2,
        compiler_params=params(),
        name="place",
    )(edge_owner.reshape(edges // LANES, LANES), edge_row.reshape(edges // LANES, LANES), counts_row)

    paper_place = place_slots(next_owner, fcap, n)
    paper_asked = jnp.zeros((n * fcap,), I32).at[paper_place].set(next_row).reshape(n, fcap)
    wanted = all_to_all(jnp.concatenate([asked_row, asked_seed, paper_asked], axis=1))
    rows = wanted[:, :cap].reshape(blocks, LANES)
    slot_seed = wanted[:, cap : 2 * cap].reshape(blocks, LANES)
    paper_rows = all_to_all(jnp.take(paper_table, wanted[:, 2 * cap :], axis=0, mode="clip"))
    next_feats = jnp.take(paper_rows.reshape(n * fcap, width), paper_place, axis=0, mode="clip")

    partial_agg = pl.pallas_call(
        functools.partial(fetch_kernel, cap, places),
        out_shape=jax.ShapeDtypeStruct((n, emb, seeds), F32),
        in_specs=[VM] * 3,
        out_specs=VM,
        scratch_shapes=[pltpu.VMEM((2 * emb, n_rows), BF16)],
        compiler_params=params(),
        name="fetch",
    )(rows, slot_seed, table)

    sems = [pltpu.SemaphoreType.DMA((len(steps),)) for _ in range(2)]
    wires = [BF16 if (axis, w) == (0, 2) else F32 for axis, w in steps]
    agg_sum = pl.pallas_call(
        functools.partial(reduce_kernel, n, steps, wires),
        out_shape=jax.ShapeDtypeStruct((emb, seeds), F32),
        in_specs=[VM],
        out_specs=VM,
        scratch_shapes=rs_scratch(n, (emb, seeds), wires) + sems,
        compiler_params=params(collective_id=1, has_side_effects=True),
        name="sum_agg",
    )(partial_agg)

    tiles = hidden // LANES
    chunk = -(-(feat_w + emb) * tiles // (n * 16)) * 16
    parts, dagg = pl.pallas_call(
        layer_kernel,
        out_shape=[
            jax.ShapeDtypeStruct((n, chunk, LANES), F32),
            jax.ShapeDtypeStruct((emb, seeds), BF16),
        ],
        in_specs=[VM] * 6,
        out_specs=[VM] * 2,
        compiler_params=params(),
        name="layer",
    )(agg_sum, counts_row, feats, w_self, w_rel, cotangent)

    wires = [BF16 if axis == 0 and w > 1 else F32 for axis, w in steps]
    all_dagg, grads = pl.pallas_call(
        functools.partial(exchange_kernel, n, steps, wires),
        out_shape=[
            jax.ShapeDtypeStruct((n, emb, seeds), BF16),
            jax.ShapeDtypeStruct((n, chunk, LANES), BF16),
        ],
        in_specs=[VM] * 2,
        out_specs=[VM] * 2,
        scratch_shapes=rs_scratch(n, (chunk, LANES), wires) + sems * 3,
        compiler_params=params(collective_id=2, has_side_effects=True),
        name="exchange",
    )(parts, dagg)
    grads = grads.reshape(n // tiles, tiles, chunk, LANES).transpose(0, 2, 1, 3)
    grads = grads.reshape(n // tiles * chunk, hidden).astype(F32)
    grad_self, grad_rel = grads[:feat_w], grads[feat_w : feat_w + emb]

    size = min(256, n_rows)
    whole = lambda shape: pl.BlockSpec(shape, lambda i: (0,) * len(shape))
    by_row = pl.BlockSpec((size, emb), lambda i: (i, 0))
    new_table, new_moment1, new_moment2 = pl.pallas_call(
        functools.partial(adam_kernel, cap, places),
        out_shape=[jax.ShapeDtypeStruct((n_rows, emb), F32)] * 3,
        grid=(n_rows // size,),
        in_specs=[whole((blocks, LANES))] * 2 + [whole((n, emb, seeds))] + [by_row] * 3,
        out_specs=[by_row] * 3,
        scratch_shapes=[
            pltpu.VMEM((2 * emb, blocks * LANES), BF16),
            pltpu.VMEM((size, blocks * LANES), BF16),
        ],
        compiler_params=params(),
        name="adam",
    )(rows, slot_seed, all_dagg, table, moment1, moment2)
    return (new_table, new_moment1, new_moment2, grad_self, grad_rel, next_feats)


def solution(mesh):
    both = P(("dp", "mp"), None)
    flat = P(("dp", "mp"))
    in_specs = (both, both, flat, flat, both, both, both, P(), P(), both, both, flat, both)
    out_specs = (both, both, both, P(), P(), both)
    return jax.shard_map(shards, mesh=mesh, in_specs=in_specs, out_specs=out_specs, check_vma=False)
```

time: 351 us -> 154 us (0.44)
  waiting for transfers between devices: 175 us -> 0.01 us
  Pallas kernels: 0 us -> 118 us
  other arithmetic: 76.6 us -> 3 us
  local copies, waits for them, and re-layouts: 48.5 us -> 14 us
  starting transfers between devices: 25.9 us -> 3.44 us
  blocking collectives: 0 us -> 14.5 us
  between operations: 14.4 us -> 0.86 us
  matrix products: 7.9 us -> 0 us
    psum x1 -> x0, waiting for transfers between devices: 128 us -> none  [shards(): grad_self, grad_rel = lax.psum((part_self, part_rel), ('dp', 'mp'))]
    pallas_call x0 -> x6, Pallas kernels: none -> 118 us  [the longest x1 65.5 us: shards(): pl.pallas_call(functools.partial(exchange_kernel, n, steps, wires), out_s...]
    scatter-add x2 -> x0, other arithmetic: 49.2 us -> none  [the longest x1 26.3 us: shards(): row_grad = jnp.zeros(table.shape, jnp.float32).at[safe_rows].add(jnp.wher...]
    all_to_all x5 -> x1, waiting for transfers between devices: 46.1 us -> 0.01 us  [all_to_all(): lax.all_to_all(x, ('dp', 'mp'), split_axis=0, concat_axis=0, tiled=True)]
    all_to_all x5 -> x1, starting transfers between devices: 25.9 us -> 3.44 us  [all_to_all(): lax.all_to_all(x, ('dp', 'mp'), split_axis=0, concat_axis=0, tiled=True)]
    gather x4 -> x2, local copies, waits for them, and re-layouts: 25.5 us -> 4.62 us  [the longest x1 2.69 us: shards(): jnp.take(paper_rows.reshape(n * fcap, width), paper_place, axis=0, mode='...]
    scatter x3 -> x1, local copies, waits for them, and re-layouts: 17.1 us -> 1.1 us  [shards(): jnp.zeros((n * fcap,), I32).at[paper_place].set(next_row).reshape(n, fcap)]
    all_to_all x0 -> x1, blocking collectives: none -> 14.5 us  [all_to_all(): lax.all_to_all(x, ('dp', 'mp'), split_axis=0, concat_axis=0, tiled=True)]
  transfers between devices with their start and end apart: 6 -> 1, of which waited for: 3 -> 0; matrix products, arithmetic and copies ran while one was open for 24% -> 4% of each run, Pallas kernels for 0% -> 76%
where the time goes in v1:
time: 154 us; the launch traced here: 153 us
  Pallas kernels  118 us (77%)
  blocking collectives  14.5 us (9%)
  local copies, waits for them, and re-layouts  14 us (9%)
  starting transfers between devices  3.44 us (2%)
  other arithmetic  3 us (2%)
    pallas_call x1, Pallas kernels, shards(): pl.pallas_call(functools.partial(exchange_kernel, n, steps, wires), out_s...  65.5 us
    pallas_call x1, Pallas kernels, shards(): pl.pallas_call(functools.partial(reduce_kernel, n, steps, wires), out_sha...  28.7 us
    all_to_all x1, blocking collectives, all_to_all(): lax.all_to_all(x, ('dp', 'mp'), split_axis=0, concat_axis=0, tiled=True)  14.5 us
    pallas_call x1, Pallas kernels, shards(): pl.pallas_call(functools.partial(fetch_kernel, cap, places), out_shape=ja...  11.5 us
    pallas_call x1, Pallas kernels, shards(): pl.pallas_call(functools.partial(adam_kernel, cap, places), out_shape=[ja...  8.39 us
    all_to_all x1, starting transfers between devices, all_to_all(): lax.all_to_all(x, ('dp', 'mp'), split_axis=0, concat_axis=0, tiled=True)  3.44 us
  transfers between devices with their start and end apart: 1, of which 0 were waited for; matrix products, arithmetic and copies ran while one was open for 4% of the time, Pallas kernels for 76%

profile of v1, /device:TPU:0, one launch (start us, length us, event | category | flops | bytes accessed | tf_op | source)
XLA Modules:
  0.0 153.4 jit_solution(10125753424695434127)
XLA Ops:
  0.6 0.0 copy-start
  0.7 0.9 fusion
  1.6 0.2 reduce_window_sum.11
  1.7 0.8 select_reduce_fusion
  2.6 0.7 fusion.4
  3.2 1.1 scatter_custom_fusion
  4.3 0.1 reshape.40
  4.4 0.7 copy-done.8
  5.1 0.7 copy-done.9
  5.8 0.7 copy-done.10
  6.5 0.5 place.1
  7.0 0.1 copy.21
  7.1 14.5 %all_to_all.17 = s32[32,1,264]{2,1,0:T(1,128)S(1)} all-to-all(s32[32,1,264]{2,1,0:T(1,128)S(1)} %copy.21), channel_id=1, replica_groups=mesh['dp'=8,'mp'=4] {'dp','mp'}, dimensions={0} | all-to-all | bytes 67584 | tf_op jit(solution)/shard_map/all_to_all | solution.py:278
  21.6 0.1 reshape.46
  21.7 1.9 %gather_fusion = bf16[256,768]{1,0:T(8,128)(2,1)} fusion(bf16[1024,768]{1,0:T(8,128)(2,1)S(1)} %copy-done, s32[1024]{0:T(1024)S(1)} %pad_clamp_fusion.1), kind=kCustom, calls=%fused_computation | custom fusion | bytes 787456 | tf_op jit(solution)/shard_map/jit(_take)/gather | solution.py:324
  23.7 3.4 %all-to-all-start.1 = ((bf16[32,8,768]{2,1,0:T(8,128)(2,1)}), bf16[32,8,768]{2,1,0:T(8,128)(2,1)}, u32[]{:S(2)}, u32[]{:S(2)}) async-start(bf16[32,8,768]{2,1,0:T(8,128)(2,1)} %bitcast.39), calls=%async_computation.1 | async-start | bytes 786432 | tf_op jit(solution)/shard_map/all_to_all | solution.py:278
  27.1 0.0 copy-start.2
  27.1 0.0 copy-start.7
  27.2 11.5 %fetch.1.x = f32[32,128,128]{2,1,0:T(8,128)S(1)} custom-call(s32[32,128]{1,0:T(8,128)S(1)} %get-tuple-element.25.rows, s32[32,128]{1,0:T(8,128)S(1)} %get-tuple-element.24.seed, f32[2048,128]{1,0:T(8,128)S(1)} %copy-done.1), custom_call_target="tpu_custom_call" | custom-call | tf_op jit(solution)/shard_map/fetch/pallas_call | solution.py:327
  38.7 28.7 %sum_agg.1.agg_sum = f32[128,128]{1,0:T(8,128)S(1)} custom-call(f32[32,128,128]{2,1,0:T(8,128)S(1)} %fetch.1.x), custom_call_target="tpu_custom_call" | custom-call | tf_op jit(solution)/shard_map/sum_agg/pallas_call | solution.py:339
  67.4 0.0 copy-done.5
  67.4 3.0 %layer.1 = (f32[32,224,128]{2,1,0:T(8,128)}, bf16[128,128]{1,0:T(8,128)(2,1)S(1)}) custom-call(f32[128,128]{1,0:T(8,128)S(1)} %sum_agg.1.agg_sum, s32[1,128]{1,0:T(1,128)S(1)} %bitcast.35, bf16[128,768]{1,0:T(8,128)(2,1)S(1)} %copy-done.7, bf16[768,1024]{1,0:T(8,128)(2,1)S(1)} %copy-done.2, bf16[128,1024]{1,0:T(8,128)(2,1)S(1)} %copy-done.6, ...), custom_call_target="tpu_custom_call" | custom-call | tf_op jit(solution)/shard_map/layer/pallas_call | solution.py:351
  70.4 65.5 %exchange.1 = (bf16[32,128,128]{2,1,0:T(8,128)(2,1)S(1)}, bf16[32,224,128]{2,1,0:T(8,128)(2,1)S(1)}) custom-call(f32[32,224,128]{2,1,0:T(8,128)} %get-tuple-element.17.grads, bf16[128,128]{1,0:T(8,128)(2,1)S(1)} %get-tuple-element.18.dagg), custom_call_target="tpu_custom_call" | custom-call | tf_op jit(solution)/shard_map/exchange/pallas_call | solution.py:364
  135.9 0.4 convert_bitcast_fusion
  136.4 2.1 %copy.22 = f32[4,224,8,128]{3,2,1,0:T(8,128)S(1)} copy(f32[4,224,8,128]{3,1,2,0:T(8,128)S(1)} %convert_bitcast_fusion) | data formatting | bytes 7340032 | tf_op jit(solution)/shard_map/convert_element_type | solution.py:377
  138.5 0.9 copy.27
  139.4 0.8 slice.27
  140.2 2.0 %slice.26 = f32[768,1024]{1,0:T(8,128)} slice(f32[896,1024]{1,0:T(8,128)S(1)} %bitcast.37), slice={[0:768], [0:1024]} | slice | bytes 6291456 | tf_op jit(solution)/shard_map/slice | solution.py:378
  142.3 0.1 copy-done.4
  142.3 8.4 %adam.1 = (f32[2048,128]{1,0:T(8,128)}, f32[2048,128]{1,0:T(8,128)}, f32[2048,128]{1,0:T(8,128)}) custom-call(s32[32,128]{1,0:T(8,128)S(1)} %get-tuple-element.25.rows, s32[32,128]{1,0:T(8,128)S(1)} %get-tuple-element.24.seed, bf16[32,128,128]{2,1,0:T(8,128)(2,1)S(1)} %get-tuple-element.19.dagg, f32[2048,128]{1,0:T(8,128)S(1)} %copy-done.1, ...), custom_call_target="tpu_custom_call" | custom-call | tf_op jit(solution)/shard_map/adam/pallas_call | solution.py:383
  150.7 0.0 all-to-all-done.1
  150.7 2.7 %gather_fusion.1 = bf16[128,768]{1,0:T(8,128)(2,1)} fusion(bf16[256,768]{1,0:T(8,128)(2,1)} %bitcast.10, s32[1024]{0:T(1024)S(1)} %pad_clamp_fusion), kind=kCustom, calls=%fused_computation.1 | custom fusion | bytes 393728 | tf_op jit(solution)/shard_map/jit(_take)/gather | solution.py:325
  (22 shorter events, 0.1 us)
Async XLA Ops:
  0.6 21.1 %copy-start = (bf16[1024,768]{1,0:T(8,128)(2,1)S(1)}, bf16[1024,768]{1,0:T(8,128)(2,1)}, u32[]{:S(2)}) copy-start(bf16[1024,768]{1,0:T(8,128)(2,1)} %param.25) | copy-start | bytes 4718596
  0.6 26.5 %copy-start.1 = (f32[2048,128]{1,0:T(8,128)S(1)}, f32[2048,128]{1,0:T(8,128)}, u32[]{:S(2)}) copy-start(f32[2048,128]{1,0:T(8,128)} %table.3) | copy-start | bytes 3145732
  4.4 0.7 copy-start.8
  5.1 0.7 copy-start.9
  5.8 0.7 copy-start.10
  23.7 43.7 %copy-start.5 = (f32[128,1024]{1,0:T(8,128)S(1)}, f32[128,1024]{1,0:T(8,128)}, u32[]{:S(2)}) copy-start(f32[128,1024]{1,0:T(8,128)} %cot.1) | copy-start | bytes 1572868
  23.7 43.7 %copy-start.6 = (bf16[128,1024]{1,0:T(8,128)(2,1)S(1)}, bf16[128,1024]{1,0:T(8,128)(2,1)}, u32[]{:S(2)}) copy-start(bf16[128,1024]{1,0:T(8,128)(2,1)} %w_rel.1) | copy-start | bytes 786436
  23.7 43.7 %copy-start.11 = (s32[128]{0:T(128)S(1)}, s32[128]{0:T(128)}, u32[]{:S(2)}) copy-start(s32[128]{0:T(128)} %param.16) | copy-start | bytes 1540
  23.7 127.1 %all-to-all-start.1 = ((bf16[32,8,768]{2,1,0:T(8,128)(2,1)}), bf16[32,8,768]{2,1,0:T(8,128)(2,1)}, u32[]{:S(2)}, u32[]{:S(2)}) async-start(bf16[32,8,768]{2,1,0:T(8,128)(2,1)} %bitcast.39), calls=%async_computation.1 | async-start | bytes 786432 | tf_op jit(solution)/shard_map/all_to_all | solution.py:278
  27.1 40.3 %copy-start.2 = (bf16[768,1024]{1,0:T(8,128)(2,1)S(1)}, bf16[768,1024]{1,0:T(8,128)(2,1)}, u32[]{:S(2)}) copy-start(bf16[768,1024]{1,0:T(8,128)(2,1)} %w_self.1) | copy-start | bytes 4718596
  27.1 40.3 %copy-start.7 = (bf16[128,768]{1,0:T(8,128)(2,1)S(1)}, bf16[128,768]{1,0:T(8,128)(2,1)}, u32[]{:S(2)}) copy-start(bf16[128,768]{1,0:T(8,128)(2,1)} %feats.1) | copy-start | bytes 589828
  140.2 2.0 %copy-start.3 = (f32[2048,128]{1,0:T(8,128)S(1)}, f32[2048,128]{1,0:T(8,128)}, u32[]{:S(2)}) copy-start(f32[2048,128]{1,0:T(8,128)} %m1.1) | copy-start | bytes 3145732
  140.2 2.1 %copy-start.4 = (f32[2048,128]{1,0:T(8,128)S(1)}, f32[2048,128]{1,0:T(8,128)}, u32[]{:S(2)}) copy-start(f32[2048,128]{1,0:T(8,128)} %m2.1) | copy-start | bytes 3145732

commit v2 on v1

v2 whole, which is shorter than its diff:
```python
import functools

import jax
import jax.numpy as jnp
from jax import lax
from jax.experimental import pallas as pl
from jax.experimental.pallas import tpu as pltpu
from jax.sharding import PartitionSpec as P

F32, BF16, I32 = jnp.float32, jnp.bfloat16, jnp.int32
LANES = 128
VMEM_LIMIT = 48 * 1024 * 1024
MESH = pl.DeviceIdType.MESH
VM = pl.BlockSpec(memory_space=pltpu.VMEM)


def dot_nt(a, b):
    return lax.dot_general(a, b, (((1,), (1,)), ((), ())), preferred_element_type=F32)


def dot_nn(a, b):
    return jnp.dot(a, b, preferred_element_type=F32)


def split(x):
    hi = x.astype(BF16)
    return hi, (x - hi.astype(F32)).astype(BF16)


def onehot(mask):
    return jnp.where(mask, 1.0, 0.0).astype(BF16)


def orders_of(n_dp, n_mp):
    core, *chips = [(0, 1 << b) for b in range(n_dp.bit_length() - 1)]
    lines = [(1, 1 << b) for b in range(n_mp.bit_length() - 1)]
    h = len(chips) // 2
    return [core, *chips, *lines], [core, *chips[h:], *chips[:h], *lines]


def position_of(device, n_mp, steps):
    coords = (device // n_mp, device % n_mp)
    pos = 0
    for axis, w in steps:
        pos = pos * 2 + (coords[axis] // w) % 2
    return pos


def partners(steps):
    coords = (lax.axis_index("dp"), lax.axis_index("mp"))
    found = []
    for axis, w in steps:
        bit = lax.rem(coords[axis] // w, 2)
        other = coords[axis] + w * (1 - 2 * bit)
        found.append((bit, (other, coords[1]) if axis == 0 else (coords[0], other)))
    return found


def enter(found):
    barrier = pltpu.get_barrier_semaphore()
    for _, device in found:
        pl.semaphore_signal(barrier, inc=1, device_id=device, device_id_type=MESH)
    pl.semaphore_wait(barrier, len(found))


def my_position(found):
    pos = 0
    for bit, _ in found:
        pos = pos * 2 + bit
    return pos


def pieces_of(rows, count):
    groups, at, found = rows // 16, 0, []
    for i in range(count):
        size = (groups // count + (i < groups % count)) * 16
        found.append((at, size))
        at += size
    return found


def sems(steps):
    return [pltpu.SemaphoreType.DMA((len(steps),)) for _ in range(2)]


def rs_scratch(n, block, steps, narrow):
    shapes = sems(steps)
    for s, step in enumerate(steps):
        half = n >> (s + 1)
        shapes += [pltpu.VMEM((half, *block), BF16 if narrow(step) else F32)]
        shapes += [pltpu.VMEM((half, *block), F32)]
        shapes += [pltpu.VMEM((half, *block) if narrow(step) else (1, 16, LANES), BF16)]
    return shapes


def rs_chain(x, n, steps, found, narrow, scratch):
    send, recv = scratch[:2]
    cur = x
    for s, (bit, device) in enumerate(found):
        half = n >> (s + 1)
        arrive, total, rounded = scratch[2 + 3 * s : 5 + 3 * s]
        away, keep = (1 - bit) * half, bit * half
        src = cur.at[pl.ds(away, half)]
        if narrow(steps[s]):
            src = rounded

            @pl.loop(0, half)
            def _(i, cur=cur, rounded=rounded, away=away):
                rounded[i] = cur[away + i].astype(BF16)

        copy = pltpu.make_async_remote_copy(
            src_ref=src, dst_ref=arrive, send_sem=send.at[s], recv_sem=recv.at[s],
            device_id=device, device_id_type=MESH,
        )
        copy.start()
        yield
        copy.wait()

        @pl.loop(0, half)
        def _(i, cur=cur, total=total, arrive=arrive, keep=keep):
            total[i] = cur[keep + i] + arrive[i].astype(F32)

        cur = total
    return cur


def ag_chain(out, n, found, scratch):
    send, recv = scratch
    pos = my_position(found)
    for s in reversed(range(len(found))):
        size = n >> (s + 1)
        here = out.at[pl.ds((pos // size) * size, size)]
        copy = pltpu.make_async_remote_copy(
            src_ref=here, dst_ref=here, send_sem=send.at[s], recv_sem=recv.at[s],
            device_id=found[s][1], device_id_type=MESH,
        )
        copy.start()
        yield
        copy.wait()


def run(chains):
    while chains:
        left = []
        for chain in chains:
            try:
                next(chain)
                left.append(chain)
            except StopIteration:
                pass
        chains = left


def reduce_kernel(n, orders, narrow, xs, out, *scratch):
    found = [partners(steps) for steps in orders]
    enter(found[0])
    per = len(scratch) // len(xs)
    starts = [0]
    for x in xs:
        starts.append(starts[-1] + x.shape[1])

    def chain(k):
        mine = scratch[k * per : (k + 1) * per]
        total = yield from rs_chain(xs[k], n, orders[k % 2], found[k % 2], narrow, mine)
        out[starts[k] : starts[k + 1], :] = total[0]

    run([chain(k) for k in range(len(xs))])


def exchange_kernel(n, orders, narrow, parts, daggs, out_daggs, out_grads, *scratch):
    found = [partners(steps) for steps in orders]
    pos = [my_position(f) for f in found]
    enter(found[0])
    count, small = len(parts), 2 * len(daggs)
    mine, rest = scratch[:small], scratch[small:]
    per = len(rest) // count

    def row_chain(k):
        out_daggs[k][pos[k % 2]] = daggs[k][...]
        yield from ag_chain(out_daggs[k], n, found[k % 2], mine[2 * k : 2 * k + 2])

    def grad_chain(k):
        own = rest[k * per : (k + 1) * per]
        total = yield from rs_chain(parts[k], n, orders[k % 2], found[k % 2], narrow, own[2:])
        out_grads[k][pos[k % 2]] = total[0].astype(BF16)
        yield from ag_chain(out_grads[k], n, found[k % 2], own[:2])

    run([grad_chain(k) for k in range(count)] + [row_chain(k) for k in range(len(daggs))])


def place_kernel(
    n, cap, fcap, slots_per, owner, row, counts, p_owner, p_row, out_row, out_seed, out_asked, out_place
):
    blocks = owner.shape[0]
    seeds = counts.shape[1]
    per = LANES // slots_per
    at_seed = lax.broadcasted_iota(I32, (blocks, seeds), 1)
    at_block = lax.broadcasted_iota(I32, (blocks, seeds), 0)
    spread = jnp.where(at_seed // per == at_block, counts[...].astype(F32), 0.0).astype(BF16)
    s_i = lax.broadcasted_iota(I32, (seeds, LANES), 0)
    l_i = lax.broadcasted_iota(I32, (seeds, LANES), 1)
    count = dot_nn(spread, onehot(lax.rem(s_i, per) == l_i // slots_per))
    lane = lax.broadcasted_iota(I32, (blocks, LANES), 1)
    live = lax.rem(lane, slots_per).astype(F32) < count - 0.5
    wanted = jnp.where(live, row[...] + 1, 0)
    seed = lax.broadcasted_iota(I32, (blocks, LANES), 0) * per + lane // slots_per
    parts = [(wanted // 64).astype(F32), lax.rem(wanted, 64).astype(F32), seed.astype(F32)]
    dev = lax.broadcasted_iota(I32, (n, LANES), 0)
    hot = [jnp.where(dev == owner[a : a + 1, :], 1.0, 0.0) for a in range(blocks)]
    t_i = lax.broadcasted_iota(I32, (LANES, LANES), 0)
    t_j = lax.broadcasted_iota(I32, (LANES, LANES), 1)
    before = dot_nn(jnp.concatenate([h.astype(BF16) for h in hot], axis=0), onehot(t_i < t_j))
    base = jnp.zeros((n, 1), F32)
    place = lax.broadcasted_iota(I32, (cap, LANES), 0).astype(F32)
    left, right = [], []
    for a in range(blocks):
        slot = jnp.sum(hot[a] * (before[a * n : (a + 1) * n] + base), axis=0, keepdims=True)
        base = base + jnp.sum(hot[a], axis=1, keepdims=True)
        right.append(onehot(place == slot))
        left.append(
            jnp.concatenate([(hot[a] * p[a : a + 1, :]).astype(BF16) for p in parts], axis=0)
        )
    got = dot_nt(jnp.concatenate(left, axis=1), jnp.concatenate(right, axis=1))
    out_row[...] = (got[:n] * 64.0 + got[n : 2 * n] - 1.0).astype(I32)
    out_seed[...] = got[2 * n :].astype(I32)
    p_hot = jnp.where(dev == p_owner[...], 1.0, 0.0)
    slot = jnp.sum(p_hot * dot_nn(p_hot.astype(BF16), onehot(t_i < t_j)), axis=0, keepdims=True)
    out_place[...] = p_owner[...] * fcap + slot.astype(I32)
    high, low = p_row[...] // 64, lax.rem(p_row[...], 64)
    pair = [(p_hot * v.astype(F32)).astype(BF16) for v in (high, low)]
    at_slot = onehot(lax.broadcasted_iota(I32, (fcap, LANES), 0).astype(F32) == slot)
    got = dot_nt(jnp.concatenate(pair, axis=0), at_slot)
    out_asked[...] = (got[:n] * 64.0 + got[n:]).astype(I32)


def pick(rows, wanted):
    at = lax.broadcasted_iota(I32, (rows.shape[0], LANES), 0)
    got = [
        lax.dot_general(
            onehot(at == wanted[i : i + 1, :]), rows, (((0,), (0,)), ((), ())),
            preferred_element_type=F32,
        )
        for i in range(wanted.shape[0])
    ]
    return jnp.concatenate(got, axis=0).astype(BF16)


def papers_kernel(wanted, papers, out):
    out[...] = pick(papers[...], wanted)


def unpack_kernel(pieces, tiles, grads, place, rows, out_self, out_rel, out_next):
    out_next[...] = pick(rows[...], place)
    chunk = sum(size for _, size in pieces)
    for (start, size), grad in zip(pieces, grads):
        for j in range(grad.shape[0]):
            top = j // tiles * chunk + start
            cols = slice(j % tiles * LANES, (j % tiles + 1) * LANES)
            first = 0
            for out in (out_self, out_rel):
                low, high = max(top, first), min(top + size, first + out.shape[0])
                if low < high:
                    out[low - first : high - first, cols] = grad[j, low - top : high - top].astype(F32)
                first += out.shape[0]


def seed_hot(seed, d, cap, seeds):
    q = LANES // cap
    lane = lax.broadcasted_iota(I32, (1, LANES), 1)
    which = seed[pl.ds(d, 1), :] + seeds * (lane // cap)
    return onehot(lax.broadcasted_iota(I32, (q * seeds, LANES), 0) == which)


def fetch_kernel(cap, places, rows, seed, table, outs, packed):
    n_rows, emb = table.shape
    seeds = outs[0].shape[2]
    q = LANES // cap
    flipped = table[...].T
    hi, lo = split(flipped)
    packed[:emb, :] = hi
    packed[emb:, :] = lo
    at = lax.broadcasted_iota(I32, (n_rows, LANES), 0)
    for d in range(0, rows.shape[0], 2):
        hot = jnp.concatenate([onehot(at == rows[d + j : d + j + 1, :]) for j in range(2)], axis=1)
        got = dot_nn(packed[...], hot)
        vals = got[:emb] + got[emb:]
        for j in range(2):
            v_hi, v_lo = split(vals[:, j * LANES : (j + 1) * LANES])
            both = dot_nt(jnp.concatenate([v_hi, v_lo], axis=0), seed_hot(seed, d + j, cap, seeds))
            sums = both[:emb] + both[emb:]
            for k in range(q):
                at_row = 0
                for p, out in enumerate(outs):
                    size = out.shape[1]
                    place = places[p % 2][(d + j) * q + k]
                    out[place] = sums[at_row : at_row + size, k * seeds : (k + 1) * seeds]
                    at_row += size


def layer_kernel(agg_sum, counts, feats, w_self, w_rel, cot, out_parts, out_daggs):
    n = out_parts[0].shape[0]
    rows = sum(out.shape[1] for out in out_parts)
    width = w_self.shape[1]
    tiles = width // LANES
    count = counts[...].astype(F32)
    agg_t = agg_sum[...] / count
    agg_b = agg_t.T.astype(BF16)
    pre = dot_nn(feats[...], w_self[...]) + dot_nn(agg_b, w_rel[...])
    sig = 1.0 / (1.0 + jnp.exp(-pre))
    dpre = (cot[...] * sig * (1.0 + pre * (1.0 - sig))).astype(BF16)
    dagg = (dot_nt(w_rel[...], dpre) / count).astype(BF16)
    half = dagg.shape[0] // 2
    for p, out in enumerate(out_daggs):
        out[...] = dagg[p * half : (p + 1) * half]
    flipped = [feats[...].astype(F32).T.astype(BF16), agg_t.astype(BF16)]
    pad = n // tiles * rows - flipped[0].shape[0] - flipped[1].shape[0]
    if pad:
        flipped.append(jnp.zeros((pad, agg_t.shape[1]), BF16))
    lhs = jnp.concatenate(flipped, axis=0)
    for i in range(n // tiles):
        got = dot_nn(lhs[i * rows : (i + 1) * rows], dpre)
        for t in range(tiles):
            at_row = 0
            for out in out_parts:
                size = out.shape[1]
                out[i * tiles + t] = got[at_row : at_row + size, t * LANES : (t + 1) * LANES]
                at_row += size


def adam_kernel(cap, places, rows, seed, daggs, table, m1, m2, o_table, o_m1, o_m2, slot_g, hot):
    size, emb = table.shape
    seeds = daggs[0].shape[2]
    q = LANES // cap
    blocks = rows.shape[0]

    @pl.when(pl.program_id(0) == 0)
    def _():
        for d in range(blocks):
            grads = [
                jnp.concatenate([g[places[p][d * q + k]] for p, g in enumerate(daggs)], axis=0)
                for k in range(q)
            ]
            got = dot_nn(jnp.concatenate(grads, axis=1), seed_hot(seed, d, cap, seeds))
            slot_g[:emb, d * LANES : (d + 1) * LANES] = got.astype(BF16)
        slot_g[emb:, :] = jnp.ones((emb, blocks * LANES), BF16)

    at = lax.broadcasted_iota(I32, (size, LANES), 0) + pl.program_id(0) * size
    for d in range(blocks):
        hot[:, d * LANES : (d + 1) * LANES] = onehot(at == rows[d : d + 1, :])
    got = dot_nt(hot[...], slot_g[...])
    grad, touched = got[:, :emb], got[:, emb:] > 0.5
    m_new = 0.9 * m1[...] + 0.1 * grad
    v_new = 0.999 * m2[...] + 0.001 * grad * grad
    step = 0.05 * (m_new / (1.0 - 0.9**10)) / (jnp.sqrt(v_new / (1.0 - 0.999**10)) + 1e-08)
    o_table[...] = jnp.where(touched, table[...] - step, table[...])
    o_m1[...] = jnp.where(touched, m_new, m1[...])
    o_m2[...] = jnp.where(touched, v_new, m2[...])


def params(**more):
    return pltpu.CompilerParams(vmem_limit_bytes=VMEM_LIMIT, **more)


def grouped(kernel, groups):
    def body(*refs):
        given, at = [], 0
        for k in groups:
            given.append(list(refs[at : at + k]) if k else refs[at])
            at += max(k, 1)
        kernel(*given, *refs[at:])

    return body


def call_grouped(kernel, ins, outs, out_shape, scratch, compiler_params, name):
    count = sum(max(k, 1) for k in ins)
    return pl.pallas_call(
        grouped(kernel, ins + outs),
        out_shape=out_shape,
        in_specs=[VM] * count,
        out_specs=[VM] * len(out_shape),
        scratch_shapes=scratch,
        compiler_params=compiler_params,
        name=name,
    )


def all_to_all(x):
    return lax.all_to_all(x, ("dp", "mp"), split_axis=0, concat_axis=0, tiled=True)


def shards(
    feats,
    edge_owner,
    edge_row,
    counts,
    table,
    moment1,
    moment2,
    w_self,
    w_rel,
    cotangent,
    next_owner,
    next_row,
    paper_table,
):
    n_dp, n_mp = lax.axis_size("dp"), lax.axis_size("mp")
    n = n_dp * n_mp
    orders = orders_of(n_dp, n_mp)
    places = [[position_of(d, n_mp, steps) for d in range(n)] for steps in orders]
    seeds = counts.shape[0]
    edges = edge_row.shape[0]
    n_rows, emb = table.shape
    feat_w, hidden = w_self.shape
    width = paper_table.shape[1]
    cap = max(2, 2 * edges // n)
    fcap = max(2, 2 * seeds // n)
    blocks = n * cap // LANES
    counts_row = counts.reshape(1, seeds)
    shape = jax.ShapeDtypeStruct

    asked_row, asked_seed, asked_paper, paper_place = pl.pallas_call(
        functools.partial(place_kernel, n, cap, fcap, edges // seeds),
        out_shape=[shape((n, cap), I32)] * 2 + [shape((n, fcap), I32), shape((1, seeds), I32)],
        in_specs=[VM] * 5,
        out_specs=[VM] * 4,
        compiler_params=params(),
        name="place",
    )(
        edge_owner.reshape(edges // LANES, LANES),
        edge_row.reshape(edges // LANES, LANES),
        counts_row,
        next_owner.reshape(1, seeds),
        next_row.reshape(1, seeds),
    )

    wanted = all_to_all(jnp.concatenate([asked_row, asked_seed, asked_paper], axis=1))
    rows = wanted[:, :cap].reshape(blocks, LANES)
    slot_seed = wanted[:, cap : 2 * cap].reshape(blocks, LANES)
    answer = pl.pallas_call(
        papers_kernel,
        out_shape=shape((n * fcap, width), BF16),
        in_specs=[VM] * 2,
        out_specs=VM,
        compiler_params=params(),
        name="papers",
    )(wanted[:, 2 * cap :].reshape(n * fcap // LANES, LANES), paper_table)
    paper_rows = all_to_all(answer.reshape(n, fcap, width)).reshape(n * fcap, width)

    sizes = [size for _, size in pieces_of(emb, 4)]
    partial_agg = call_grouped(
        functools.partial(fetch_kernel, cap, places),
        (0, 0, 0),
        (len(sizes),),
        [shape((n, size, seeds), F32) for size in sizes],
        [pltpu.VMEM((2 * emb, n_rows), BF16)],
        params(),
        "fetch",
    )(rows, slot_seed, table)

    narrow = lambda step: step[0] == 0 and step[1] > 1
    scratch = []
    for k, size in enumerate(sizes):
        scratch += rs_scratch(n, (size, seeds), orders[k % 2], narrow)
    agg_sum = call_grouped(
        functools.partial(reduce_kernel, n, orders, narrow),
        (len(sizes),),
        (0,),
        [shape((emb, seeds), F32)],
        scratch,
        params(collective_id=1, has_side_effects=True),
        "sum_agg",
    )(*partial_agg)[0]

    tiles = hidden // LANES
    chunk = -(-(feat_w + emb) * tiles // (n * 16)) * 16
    pieces = pieces_of(chunk, 4)
    out = call_grouped(
        layer_kernel,
        (0,) * 6,
        (4, 2),
        [shape((n, size, LANES), F32) for _, size in pieces]
        + [shape((emb // 2, seeds), BF16)] * 2,
        [],
        params(),
        "layer",
    )(agg_sum, counts_row, feats, w_self, w_rel, cotangent)

    narrow = lambda step: step[0] == 1 or step[1] > 1
    scratch = sems(orders[0]) * 2
    for k, (_, size) in enumerate(pieces):
        scratch += sems(orders[0]) + rs_scratch(n, (size, LANES), orders[k % 2], narrow)
    out = call_grouped(
        functools.partial(exchange_kernel, n, orders, narrow),
        (4, 2),
        (2, 4),
        [shape((n, emb // 2, seeds), BF16)] * 2
        + [shape((n, size, LANES), BF16) for _, size in pieces],
        scratch,
        params(collective_id=2, has_side_effects=True),
        "exchange",
    )(*out)
    daggs, grads = out[:2], out[2:]

    size = min(256, n_rows)
    whole = lambda shape: pl.BlockSpec(shape, lambda i: (0,) * len(shape))
    by_row = pl.BlockSpec((size, emb), lambda i: (i, 0))
    new_table, new_moment1, new_moment2 = pl.pallas_call(
        grouped(functools.partial(adam_kernel, cap, places), (0, 0, 2)),
        out_shape=[shape((n_rows, emb), F32)] * 3,
        grid=(n_rows // size,),
        in_specs=[whole((blocks, LANES))] * 2 + [whole((n, emb // 2, seeds))] * 2 + [by_row] * 3,
        out_specs=[by_row] * 3,
        scratch_shapes=[
            pltpu.VMEM((2 * emb, blocks * LANES), BF16),
            pltpu.VMEM((size, blocks * LANES), BF16),
        ],
        compiler_params=params(),
        name="adam",
    )(rows, slot_seed, *daggs, table, moment1, moment2)

    grad_self, grad_rel, next_feats = call_grouped(
        functools.partial(unpack_kernel, pieces, tiles),
        (4, 0, 0),
        (0, 0, 0),
        [shape((feat_w, hidden), F32), shape((emb, hidden), F32), shape((seeds, width), BF16)],
        [],
        params(),
        "unpack",
    )(*grads, paper_place, paper_rows)
    return (new_table, new_moment1, new_moment2, grad_self, grad_rel, next_feats)


def solution(mesh):
    both = P(("dp", "mp"), None)
    flat = P(("dp", "mp"))
    in_specs = (both, both, flat, flat, both, both, both, P(), P(), both, both, flat, both)
    out_specs = (both, both, both, P(), P(), both)
    return jax.shard_map(shards, mesh=mesh, in_specs=in_specs, out_specs=out_specs, check_vma=False)
```

time: 154 us -> 109 us (0.71)
  Pallas kernels: 118 us -> 85.2 us
  local copies, waits for them, and re-layouts: 14 us -> 5.91 us
  other arithmetic: 3 us -> 0.01 us
    pallas_call x6 -> x8, Pallas kernels: 118 us -> 85.2 us  [the longest x1 38.8 us: shards(): call_grouped(functools.partial(exchange_kernel, n, orders, narrow), (4, 2...]
    gather x2 -> x0, local copies, waits for them, and re-layouts: 4.62 us -> none  [the longest x1 2.69 us: shards(): jnp.take(paper_rows.reshape(n * fcap, width), paper_place, axis=0, mode='...]
    slice x3 -> x1, local copies, waits for them, and re-layouts: 2.88 us -> 0.01 us  [shards(): wanted[:, 2 * cap:].reshape(n * fcap // LANES, LANES)]
    unnamed x26 -> x29, local copies, waits for them, and re-layouts: 3.06 us -> 5.76 us
    convert_element_type x1 -> x0, local copies, waits for them, and re-layouts: 2.13 us -> none  [shards(): grads = grads.reshape(n // tiles * chunk, hidden).astype(F32)]
  transfers between devices with their start and end apart: 1 -> 1, of which waited for: 0 -> 0; matrix products, arithmetic and copies ran while one was open for 4% -> 0% of each run, Pallas kernels for 76% -> 74%
where the time goes in v2:
time: 109 us
  Pallas kernels  85.2 us (78%)
  blocking collectives  14.5 us (13%)
  local copies, waits for them, and re-layouts  5.91 us (5%)
  starting transfers between devices  2.6 us (2%)
    pallas_call x1, Pallas kernels, shards(): call_grouped(functools.partial(exchange_kernel, n, orders, narrow), (4, 2...  38.8 us
    pallas_call x1, Pallas kernels, shards(): call_grouped(functools.partial(reduce_kernel, n, orders, narrow), (len(si...  19.9 us
    all_to_all x1, blocking collectives, all_to_all(): lax.all_to_all(x, ('dp', 'mp'), split_axis=0, concat_axis=0, tiled=True)  14.5 us
    pallas_call x1, Pallas kernels, shards(): call_grouped(functools.partial(fetch_kernel, cap, places), (0, 0, 0), (le...  11.5 us
    pallas_call x1, Pallas kernels, shards(): pl.pallas_call(grouped(functools.partial(adam_kernel, cap, places), (0, 0...  8.42 us
    unnamed x29, local copies, waits for them, and re-layouts  5.76 us
    pallas_call x1, Pallas kernels, shards(): call_grouped(layer_kernel, (0,) * 6, (4, 2), [shape((n, size, LANES), F32...  2.61 us
    all_to_all x1, starting transfers between devices, all_to_all(): lax.all_to_all(x, ('dp', 'mp'), split_axis=0, concat_axis=0, tiled=True)  2.6 us
  transfers between devices with their start and end apart: 1, of which 0 were waited for; matrix products, arithmetic and copies ran while one was open for 0% of the time, Pallas kernels for 74%

profile of v2, /device:TPU:0, one launch (start us, length us, event | category | flops | bytes accessed | tf_op | source)
XLA Modules:
  0.0 109.1 jit_solution(17207152798805222784)
XLA Ops:
  0.6 0.0 copy-start.8
  0.6 0.7 copy-done.8
  1.3 0.7 copy-done.9
  2.0 0.7 copy-done.10
  2.7 0.7 copy-done.12
  3.3 0.7 copy-done.13
  4.0 0.7 place.1
  4.7 0.0 copy-start
  4.7 0.1 copy.19
  4.7 14.5 %all_to_all.17 = s32[32,1,264]{2,1,0:T(1,128)S(1)} all-to-all(s32[32,1,264]{2,1,0:T(1,128)S(1)} %copy.19), channel_id=1, replica_groups=mesh['dp'=8,'mp'=4] {'dp','mp'}, dimensions={0} | all-to-all | bytes 67584 | tf_op jit(solution)/shard_map/all_to_all | solution.py:389
  19.3 0.1 reshape.43.wanted
  19.3 0.0 copy-start.1
  19.4 1.4 %copy-done.1 = bf16[1024,768]{1,0:T(8,128)(2,1)S(1)} copy-done((bf16[1024,768]{1,0:T(8,128)(2,1)S(1)}, bf16[1024,768]{1,0:T(8,128)(2,1)}, u32[]{:S(2)}) %copy-start.1) | copy-done | bytes 1572888
  20.8 1.4 %papers.2 = bf16[256,768]{1,0:T(8,128)(2,1)} custom-call(s32[2,128]{1,0:T(2,128)S(1)} %reshape.43.wanted, bf16[1024,768]{1,0:T(8,128)(2,1)S(1)} %copy-done.1), custom_call_target="tpu_custom_call" | custom-call | tf_op jit(solution)/shard_map/papers/pallas_call | solution.py:440
  22.1 2.6 %all-to-all-start.1 = ((bf16[32,8,768]{2,1,0:T(8,128)(2,1)}), bf16[32,8,768]{2,1,0:T(8,128)(2,1)S(1)}, u32[]{:S(2)}, u32[]{:S(2)}) async-start(bf16[32,8,768]{2,1,0:T(8,128)(2,1)} %bitcast.6), calls=%async_computation.1 | async-start | bytes 786432 | tf_op jit(solution)/shard_map/all_to_all | solution.py:389
  24.8 0.0 copy-start.5
  24.8 0.0 copy-start.6
  24.8 0.0 copy-start.7
  24.8 0.0 copy-start.11
  24.8 11.5 %fetch.1 = (f32[32,32,128]{2,1,0:T(8,128)S(1)}, f32[32,32,128]{2,1,0:T(8,128)S(1)}, f32[32,32,128]{2,1,0:T(8,128)S(1)}, f32[32,32,128]{2,1,0:T(8,128)S(1)}) custom-call(s32[32,128]{1,0:T(8,128)S(1)} %get-tuple-element.59.refs_0_, s32[32,128]{1,0:T(8,128)S(1)} %get-tuple-element.58.refs_1_, f32[2048,128]{1,0:T(8,128)S(1)} %copy-done), custom_call_target="tpu_custom_call" | custom-call | tf_op jit(solution)/shard_map/fetch/pallas_call | solution.py:451
  36.3 19.9 %sum_agg.1.refs_0_ = f32[128,128]{1,0:T(8,128)S(1)} custom-call(f32[32,32,128]{2,1,0:T(8,128)S(1)} %get-tuple-element.35.refs_0_, f32[32,32,128]{2,1,0:T(8,128)S(1)} %get-tuple-element.36.refs_1_, f32[32,32,128]{2,1,0:T(8,128)S(1)} %get-tuple-element.37.refs_2_, f32[32,32,128]{2,1,0:T(8,128)S(1)} %get-tuple-element.38.refs_3_), custom_call_target="tpu_custom_call" | custom-call | tf_op jit(solution)/shard_map/sum_agg/pallas_call | solution.py:465
  56.2 0.0 copy-done.5
  56.2 0.0 copy-done.6
  56.2 0.0 copy-done.7
  56.2 0.0 copy-done.11
  56.2 2.6 %layer.1 = (f32[32,64,128]{2,1,0:T(8,128)S(1)}, f32[32,64,128]{2,1,0:T(8,128)S(1)}, f32[32,48,128]{2,1,0:T(8,128)S(1)}, f32[32,48,128]{2,1,0:T(8,128)S(1)}, bf16...) custom-call(f32[128,128]{1,0:T(8,128)S(1)} %sum_agg.1.refs_0_, s32[1,128]{1,0:T(1,128)S(1)} %bitcast.16, ...), custom_call_target="tpu_custom_call" | custom-call | tf_op jit(solution)/shard_map/layer/pallas_call | solution.py:478
  58.8 0.0 copy-start.2
  58.8 1.0 copy-done.2
  59.8 38.8 %exchange.1 = (bf16[32,64,128]{2,1,0:T(8,128)(2,1)S(1)}, bf16[32,64,128]{2,1,0:T(8,128)(2,1)S(1)}, bf16[32,64,128]{2,1,0:T(8,128)(2,1)S(1)}, bf16[32,64,128]{2,1...) custom-call(f32[32,64,128]{2,1,0:T(8,128)S(1)} %get-tuple-element.39.refs_0_, ...), custom_call_target="tpu_custom_call" | custom-call | tf_op jit(solution)/shard_map/exchange/pallas_call | solution.py:493
  98.6 8.4 %adam.1 = (f32[2048,128]{1,0:T(8,128)}, f32[2048,128]{1,0:T(8,128)}, f32[2048,128]{1,0:T(8,128)}) custom-call(s32[32,128]{1,0:T(8,128)S(1)} %get-tuple-element.59.refs_0_, s32[32,128]{1,0:T(8,128)S(1)} %get-tuple-element.58.refs_1_, bf16[32,64,128]{2,1,0:T(8,128)(2,1)S(1)} %get-tuple-element.45.refs_2_, bf16[32,64,128]{2,1,0:T(8,128)(2,1)S(1)} %get-tuple-element.46.refs_3_, ...), custom_call_target="tpu_custom_call" | custom-call | tf_op jit(solution)/shard_map/adam/pallas_call | solution.py:508
  107.0 0.0 all-to-all-done.1
  107.0 2.1 %unpack.1 = (f32[768,1024]{1,0:T(8,128)}, f32[128,1024]{1,0:T(8,128)}, bf16[128,768]{1,0:T(8,128)(2,1)}) custom-call(bf16[32,64,128]{2,1,0:T(8,128)(2,1)S(1)} %get-tuple-element.50.refs_0_, bf16[32,64,128]{2,1,0:T(8,128)(2,1)S(1)} %get-tuple-element.51.refs_1_, bf16[32,48,128]{2,1,0:T(8,128)(2,1)S(1)} %get-tuple-element.52.refs_2_, ...), custom_call_target="tpu_custom_call" | custom-call | tf_op jit(solution)/shard_map/unpack/pallas_call | solution.py:522
  (13 shorter events, 0.0 us)
Async XLA Ops:
  0.6 0.7 copy-start.8
  1.3 0.7 copy-start.9
  2.0 0.7 copy-start.10
  2.7 0.7 copy-start.12
  3.3 0.7 copy-start.13
  4.7 20.1 %copy-start = (f32[2048,128]{1,0:T(8,128)S(1)}, f32[2048,128]{1,0:T(8,128)}, u32[]{:S(2)}) copy-start(f32[2048,128]{1,0:T(8,128)} %refs_4_.3) | copy-start | bytes 3145732
  19.3 1.4 %copy-start.1 = (bf16[1024,768]{1,0:T(8,128)(2,1)S(1)}, bf16[1024,768]{1,0:T(8,128)(2,1)}, u32[]{:S(2)}) copy-start(bf16[1024,768]{1,0:T(8,128)(2,1)} %papers.3) | copy-start | bytes 4718596
  22.1 84.9 %all-to-all-start.1 = ((bf16[32,8,768]{2,1,0:T(8,128)(2,1)}), bf16[32,8,768]{2,1,0:T(8,128)(2,1)S(1)}, u32[]{:S(2)}, u32[]{:S(2)}) async-start(bf16[32,8,768]{2,1,0:T(8,128)(2,1)} %bitcast.6), calls=%async_computation.1 | async-start | bytes 786432 | tf_op jit(solution)/shard_map/all_to_all | solution.py:389
  24.8 31.4 %copy-start.5 = (f32[128,1024]{1,0:T(8,128)S(1)}, f32[128,1024]{1,0:T(8,128)}, u32[]{:S(2)}) copy-start(f32[128,1024]{1,0:T(8,128)} %refs_5_.2) | copy-start | bytes 1572868
  24.8 31.4 %copy-start.6 = (bf16[128,1024]{1,0:T(8,128)(2,1)S(1)}, bf16[128,1024]{1,0:T(8,128)(2,1)}, u32[]{:S(2)}) copy-start(bf16[128,1024]{1,0:T(8,128)(2,1)} %refs_4_.2) | copy-start | bytes 786436
  24.8 31.4 %copy-start.7 = (bf16[128,768]{1,0:T(8,128)(2,1)S(1)}, bf16[128,768]{1,0:T(8,128)(2,1)}, u32[]{:S(2)}) copy-start(bf16[128,768]{1,0:T(8,128)(2,1)} %refs_2_.3) | copy-start | bytes 589828
  24.8 31.4 %copy-start.11 = (s32[128]{0:T(128)S(1)}, s32[128]{0:T(128)}, u32[]{:S(2)}) copy-start(s32[128]{0:T(128)} %param.16) | copy-start | bytes 1540
  58.8 1.0 copy-start.2
  59.8 38.8 %copy-start.3 = (f32[2048,128]{1,0:T(8,128)S(1)}, f32[2048,128]{1,0:T(8,128)}, u32[]{:S(2)}) copy-start(f32[2048,128]{1,0:T(8,128)} %refs_5_.3) | copy-start | bytes 3145732
  59.8 38.8 %copy-start.4 = (f32[2048,128]{1,0:T(8,128)S(1)}, f32[2048,128]{1,0:T(8,128)}, u32[]{:S(2)}) copy-start(f32[2048,128]{1,0:T(8,128)} %refs_6_.1) | copy-start | bytes 3145732

commit v3 on v2

--- a/solution.py
+++ b/solution.py
@@ -35,7 +35,8 @@
     core, *chips = [(0, 1 << b) for b in range(n_dp.bit_length() - 1)]
     lines = [(1, 1 << b) for b in range(n_mp.bit_length() - 1)]
     h = len(chips) // 2
-    return [core, *chips, *lines], [core, *chips[h:], *chips[:h], *lines]
+    chips = [[*chips, *lines], [*chips[h:], *chips[:h], *lines], [*lines, *chips]]
+    return [[core, *order] for order in chips]
 
 
 def position_of(device, n_mp, steps):
@@ -44,6 +45,10 @@
     for axis, w in steps:
         pos = pos * 2 + (coords[axis] // w) % 2
     return pos
+
+
+def order_at(k):
+    return 2 if k == 4 else k % 2
 
 
 def partners(steps):
@@ -167,30 +172,67 @@
     run([chain(k) for k in range(len(xs))])
 
 
-def exchange_kernel(n, orders, narrow, parts, daggs, out_daggs, out_grads, *scratch):
+def exchange_kernel(
+    n, orders, narrow, cap, places, parts, daggs, rows, seed, out_got, out_grads, *scratch
+):
     found = [partners(steps) for steps in orders]
     pos = [my_position(f) for f in found]
     enter(found[0])
     count, small = len(parts), 2 * len(daggs)
+    slot_g, hot, *arrived = scratch[: 2 + len(daggs)]
+    scratch = scratch[2 + len(daggs) :]
     mine, rest = scratch[:small], scratch[small:]
     per = len(rest) // count
 
     def row_chain(k):
-        out_daggs[k][pos[k % 2]] = daggs[k][...]
-        yield from ag_chain(out_daggs[k], n, found[k % 2], mine[2 * k : 2 * k + 2])
+        arrived[k][pos[k % 2]] = daggs[k][...]
+        yield from ag_chain(arrived[k], n, found[k % 2], mine[2 * k : 2 * k + 2])
 
     def grad_chain(k):
         own = rest[k * per : (k + 1) * per]
-        total = yield from rs_chain(parts[k], n, orders[k % 2], found[k % 2], narrow, own[2:])
-        out_grads[k][pos[k % 2]] = total[0].astype(BF16)
-        yield from ag_chain(out_grads[k], n, found[k % 2], own[:2])
-
-    run([grad_chain(k) for k in range(count)] + [row_chain(k) for k in range(len(daggs))])
+        at = order_at(k)
+        total = yield from rs_chain(parts[k], n, orders[at], found[at], narrow, own[2:])
+        out_grads[k][pos[at]] = total[0].astype(BF16)
+        yield from ag_chain(out_grads[k], n, found[at], own[:2])
+
+    def row_grads():
+        for _ in orders[0]:
+            yield
+        blocks, size = rows.shape[0], hot.shape[0]
+        emb = slot_g.shape[0] // 2
+        seeds = arrived[0].shape[2]
+        q = LANES // cap
+        for d in range(blocks):
+            grads = [
+                jnp.concatenate([g[places[p][d * q + k]] for p, g in enumerate(arrived)], axis=0)
+                for k in range(q)
+            ]
+            got = dot_nn(jnp.concatenate(grads, axis=1), seed_hot(seed, d, cap, seeds))
+            slot_g[:emb, d * LANES : (d + 1) * LANES] = got.astype(BF16)
+        slot_g[emb:, :] = jnp.ones((emb, blocks * LANES), BF16)
+        for first in range(0, out_got.shape[0], size):
+            yield
+            at = lax.broadcasted_iota(I32, (size, LANES), 0) + first
+            for d in range(blocks):
+                hot[:, d * LANES : (d + 1) * LANES] = onehot(at == rows[d : d + 1, :])
+            out_got[first : first + size, :] = dot_nt(hot[...], slot_g[...])
+
+    chains = [grad_chain(k) for k in range(count)] + [row_chain(k) for k in range(len(daggs))]
+    run(chains + [row_grads()])
 
 
 def place_kernel(
-    n, cap, fcap, slots_per, owner, row, counts, p_owner, p_row, out_row, out_seed, out_asked, out_place
+    n, cap, fcap, slots_per, given, out_row, out_seed, out_asked, out_place, held, arrived
 ):
+    copies = [
+        pltpu.make_async_copy(src, dst, arrived.at[i])
+        for i, (src, dst) in enumerate(zip(given, held))
+    ]
+    for copy in copies:
+        copy.start()
+    for copy in copies:
+        copy.wait()
+    owner, row, counts, p_owner, p_row = held
     blocks = owner.shape[0]
     seeds = counts.shape[1]
     per = LANES // slots_per
@@ -271,29 +313,35 @@
     return onehot(lax.broadcasted_iota(I32, (q * seeds, LANES), 0) == which)
 
 
-def fetch_kernel(cap, places, rows, seed, table, outs, packed):
+def fetch_kernel(cap, places, rows, seed, table, outs, packed, hot):
     n_rows, emb = table.shape
-    seeds = outs[0].shape[2]
+    seeds = sum(out.shape[1] for out in outs)
+    blocks = rows.shape[0]
     q = LANES // cap
-    flipped = table[...].T
-    hi, lo = split(flipped)
-    packed[:emb, :] = hi
-    packed[emb:, :] = lo
-    at = lax.broadcasted_iota(I32, (n_rows, LANES), 0)
-    for d in range(0, rows.shape[0], 2):
-        hot = jnp.concatenate([onehot(at == rows[d + j : d + j + 1, :]) for j in range(2)], axis=1)
-        got = dot_nn(packed[...], hot)
-        vals = got[:emb] + got[emb:]
-        for j in range(2):
-            v_hi, v_lo = split(vals[:, j * LANES : (j + 1) * LANES])
-            both = dot_nt(jnp.concatenate([v_hi, v_lo], axis=0), seed_hot(seed, d + j, cap, seeds))
-            sums = both[:emb] + both[emb:]
+    hi, lo = split(table[...])
+    packed[:, :emb] = hi
+    packed[:, emb:] = lo
+    number = jnp.concatenate(
+        [rows[...].astype(F32), jnp.zeros((LANES - blocks, LANES), F32)], axis=0
+    ).T.astype(I32)
+    at = lax.broadcasted_iota(I32, (LANES, n_rows), 1)
+    group = hot.shape[0] // LANES
+    for first in range(0, blocks, group):
+        for j in range(group):
+            d = first + j
+            hot[j * LANES : (j + 1) * LANES, :] = onehot(at == number[:, d : d + 1])
+        got = dot_nn(hot[...], packed[...])
+        vals = got[:, :emb] + got[:, emb:]
+        for j in range(group):
+            d = first + j
+            pair = jnp.concatenate(split(vals[j * LANES : (j + 1) * LANES]), axis=1)
+            both = dot_nn(seed_hot(seed, d, cap, seeds), pair)
+            sums = both[:, :emb] + both[:, emb:]
             for k in range(q):
-                at_row = 0
+                at_row = k * seeds
                 for p, out in enumerate(outs):
                     size = out.shape[1]
-                    place = places[p % 2][(d + j) * q + k]
-                    out[place] = sums[at_row : at_row + size, k * seeds : (k + 1) * seeds]
+                    out[places[p % 2][d * q + k]] = sums[at_row : at_row + size]
                     at_row += size
 
 
@@ -303,7 +351,7 @@
     width = w_self.shape[1]
     tiles = width // LANES
     count = counts[...].astype(F32)
-    agg_t = agg_sum[...] / count
+    agg_t = agg_sum[...].T / count
     agg_b = agg_t.T.astype(BF16)
     pre = dot_nn(feats[...], w_self[...]) + dot_nn(agg_b, w_rel[...])
     sig = 1.0 / (1.0 + jnp.exp(-pre))
@@ -327,27 +375,8 @@
                 at_row += size
 
 
-def adam_kernel(cap, places, rows, seed, daggs, table, m1, m2, o_table, o_m1, o_m2, slot_g, hot):
-    size, emb = table.shape
-    seeds = daggs[0].shape[2]
-    q = LANES // cap
-    blocks = rows.shape[0]
-
-    @pl.when(pl.program_id(0) == 0)
-    def _():
-        for d in range(blocks):
-            grads = [
-                jnp.concatenate([g[places[p][d * q + k]] for p, g in enumerate(daggs)], axis=0)
-                for k in range(q)
-            ]
-            got = dot_nn(jnp.concatenate(grads, axis=1), seed_hot(seed, d, cap, seeds))
-            slot_g[:emb, d * LANES : (d + 1) * LANES] = got.astype(BF16)
-        slot_g[emb:, :] = jnp.ones((emb, blocks * LANES), BF16)
-
-    at = lax.broadcasted_iota(I32, (size, LANES), 0) + pl.program_id(0) * size
-    for d in range(blocks):
-        hot[:, d * LANES : (d + 1) * LANES] = onehot(at == rows[d : d + 1, :])
-    got = dot_nt(hot[...], slot_g[...])
+def adam_kernel(got, table, m1, m2, o_table, o_m1, o_m2):
+    emb = table.shape[1]
     grad, touched = got[:, :emb], got[:, emb:] > 0.5
     m_new = 0.9 * m1[...] + 0.1 * grad
     v_new = 0.999 * m2[...] + 0.001 * grad * grad
@@ -419,20 +448,21 @@
     counts_row = counts.reshape(1, seeds)
     shape = jax.ShapeDtypeStruct
 
+    given = [x.reshape(edges // LANES, LANES) for x in (edge_owner, edge_row)]
+    given += [counts_row, next_owner.reshape(1, seeds), next_row.reshape(1, seeds)]
     asked_row, asked_seed, asked_paper, paper_place = pl.pallas_call(
-        functools.partial(place_kernel, n, cap, fcap, edges // seeds),
+        grouped(
+            functools.partial(place_kernel, n, cap, fcap, edges // seeds),
+            (len(given), 0, 0, 0, 0, len(given)),
+        ),
         out_shape=[shape((n, cap), I32)] * 2 + [shape((n, fcap), I32), shape((1, seeds), I32)],
-        in_specs=[VM] * 5,
+        in_specs=[pl.BlockSpec(memory_space=pl.ANY)] * len(given),
         out_specs=[VM] * 4,
-        compiler_params=params(),
+        scratch_shapes=[pltpu.VMEM(x.shape, I32) for x in given]
+        + [pltpu.SemaphoreType.DMA((len(given),))],
+        compiler_params=pltpu.CompilerParams(vmem_limit_bytes=60 * 1024 * 1024),
         name="place",
-    )(
-        edge_owner.reshape(edges // LANES, LANES),
-        edge_row.reshape(edges // LANES, LANES),
-        counts_row,
-        next_owner.reshape(1, seeds),
-        next_row.reshape(1, seeds),
-    )
+    )(*given)
 
     wanted = all_to_all(jnp.concatenate([asked_row, asked_seed, asked_paper], axis=1))
     rows = wanted[:, :cap].reshape(blocks, LANES)
@@ -447,13 +477,13 @@
     )(wanted[:, 2 * cap :].reshape(n * fcap // LANES, LANES), paper_table)
     paper_rows = all_to_all(answer.reshape(n, fcap, width)).reshape(n * fcap, width)
 
-    sizes = [size for _, size in pieces_of(emb, 4)]
+    sizes = [size for _, size in pieces_of(seeds, 4)]
     partial_agg = call_grouped(
         functools.partial(fetch_kernel, cap, places),
         (0, 0, 0),
         (len(sizes),),
-        [shape((n, size, seeds), F32) for size in sizes],
-        [pltpu.VMEM((2 * emb, n_rows), BF16)],
+        [shape((n, size, emb), F32) for size in sizes],
+        [pltpu.VMEM((n_rows, 2 * emb), BF16), pltpu.VMEM((8 * LANES, n_rows), BF16)],
         params(),
         "fetch",
     )(rows, slot_seed, table)
@@ -461,12 +491,12 @@
     narrow = lambda step: step[0] == 0 and step[1] > 1
     scratch = []
     for k, size in enumerate(sizes):
-        scratch += rs_scratch(n, (size, seeds), orders[k % 2], narrow)
+        scratch += rs_scratch(n, (size, emb), orders[k % 2], narrow)
     agg_sum = call_grouped(
         functools.partial(reduce_kernel, n, orders, narrow),
         (len(sizes),),
         (0,),
-        [shape((emb, seeds), F32)],
+        [shape((seeds, emb), F32)],
         scratch,
         params(collective_id=1, has_side_effects=True),
         "sum_agg",
@@ -474,11 +504,11 @@
 
     tiles = hidden // LANES
     chunk = -(-(feat_w + emb) * tiles // (n * 16)) * 16
-    pieces = pieces_of(chunk, 4)
+    pieces = pieces_of(chunk, min(5, chunk // 16))
     out = call_grouped(
         layer_kernel,
         (0,) * 6,
-        (4, 2),
+        (len(pieces), 2),
         [shape((n, size, LANES), F32) for _, size in pieces]
         + [shape((emb // 2, seeds), BF16)] * 2,
         [],
@@ -487,41 +517,36 @@
     )(agg_sum, counts_row, feats, w_self, w_rel, cotangent)
 
     narrow = lambda step: step[0] == 1 or step[1] > 1
-    scratch = sems(orders[0]) * 2
-    for k, (_, size) in enumerate(pieces):
-        scratch += sems(orders[0]) + rs_scratch(n, (size, LANES), orders[k % 2], narrow)
-    out = call_grouped(
-        functools.partial(exchange_kernel, n, orders, narrow),
-        (4, 2),
-        (2, 4),
-        [shape((n, emb // 2, seeds), BF16)] * 2
-        + [shape((n, size, LANES), BF16) for _, size in pieces],
+    size = min(512, n_rows)
+    scratch = [pltpu.VMEM((2 * emb, blocks * LANES), BF16), pltpu.VMEM((size, blocks * LANES), BF16)]
+    scratch += [pltpu.VMEM((n, emb // 2, seeds), BF16)] * 2 + sems(orders[0]) * 2
+    for k, (_, height) in enumerate(pieces):
+        scratch += sems(orders[0]) + rs_scratch(n, (height, LANES), orders[order_at(k)], narrow)
+    got, *grads = call_grouped(
+        functools.partial(exchange_kernel, n, orders, narrow, cap, places),
+        (len(pieces), 2, 0, 0),
+        (0, len(pieces)),
+        [shape((n_rows, 2 * emb), F32)]
+        + [shape((n, height, LANES), BF16) for _, height in pieces],
         scratch,
         params(collective_id=2, has_side_effects=True),
         "exchange",
-    )(*out)
-    daggs, grads = out[:2], out[2:]
-
-    size = min(256, n_rows)
-    whole = lambda shape: pl.BlockSpec(shape, lambda i: (0,) * len(shape))
-    by_row = pl.BlockSpec((size, emb), lambda i: (i, 0))
+    )(*out, rows, slot_seed)
+
+    by_row = lambda wide: pl.BlockSpec((size, wide), lambda i: (i, 0))
     new_table, new_moment1, new_moment2 = pl.pallas_call(
-        grouped(functools.partial(adam_kernel, cap, places), (0, 0, 2)),
+        adam_kernel,
         out_shape=[shape((n_rows, emb), F32)] * 3,
         grid=(n_rows // size,),
-        in_specs=[whole((blocks, LANES))] * 2 + [whole((n, emb // 2, seeds))] * 2 + [by_row] * 3,
-        out_specs=[by_row] * 3,
-        scratch_shapes=[
-            pltpu.VMEM((2 * emb, blocks * LANES), BF16),
-            pltpu.VMEM((size, blocks * LANES), BF16),
-        ],
+        in_specs=[by_row(2 * emb)] + [by_row(emb)] * 3,
+        out_specs=[by_row(emb)] * 3,
         compiler_params=params(),
         name="adam",
-    )(rows, slot_seed, *daggs, table, moment1, moment2)
+    )(got, table, moment1, moment2)
 
     grad_self, grad_rel, next_feats = call_grouped(
         functools.partial(unpack_kernel, pieces, tiles),
-        (4, 0, 0),
+        (len(pieces), 0, 0),
         (0, 0, 0),
         [shape((feat_w, hidden), F32), shape((emb, hidden), F32), shape((seeds, width), BF16)],
         [],

time: 109 us -> 102 us (0.936)
  Pallas kernels: 85.2 us -> 79.4 us
  local copies, waits for them, and re-layouts: 5.91 us -> 3.18 us
    pallas_call x5, Pallas kernels: 52.5 us -> 48.7 us  [the longest x1 39.3 us: shards(): call_grouped(functools.partial(exchange_kernel, n, orders, narrow, cap, p...]
    unnamed x29 -> x21, local copies, waits for them, and re-layouts: 5.76 us -> 3.03 us
    pallas_call x1, Pallas kernels: 11.5 us -> 9.46 us  [shards(): call_grouped(functools.partial(fetch_kernel, cap, places), (0, 0, 0), (le...]
  transfers between devices with their start and end apart: 1 -> 1, of which waited for: 0 -> 0; matrix products, arithmetic and copies ran while one was open for 0% -> 0% of each run, Pallas kernels for 74% -> 73%
where the time goes in v3:
time: 102 us; the launch traced here: 101 us
  Pallas kernels  79.4 us (78%)
  blocking collectives  14.5 us (14%)
  local copies, waits for them, and re-layouts  3.18 us (3%)
  starting transfers between devices  2.74 us (3%)
    pallas_call x1, Pallas kernels, shards(): call_grouped(functools.partial(exchange_kernel, n, orders, narrow, cap, p...  39.3 us
    pallas_call x1, Pallas kernels, shards(): call_grouped(functools.partial(reduce_kernel, n, orders, narrow), (len(si...  19.9 us
    all_to_all x1, blocking collectives, all_to_all(): lax.all_to_all(x, ('dp', 'mp'), split_axis=0, concat_axis=0, tiled=True)  14.5 us
    pallas_call x1, Pallas kernels, shards(): call_grouped(functools.partial(fetch_kernel, cap, places), (0, 0, 0), (le...  9.46 us
    unnamed x21, local copies, waits for them, and re-layouts  3.03 us
    all_to_all x1, starting transfers between devices, all_to_all(): lax.all_to_all(x, ('dp', 'mp'), split_axis=0, concat_axis=0, tiled=True)  2.74 us
    pallas_call x1, Pallas kernels, shards(): call_grouped(layer_kernel, (0,) * 6, (len(pieces), 2), [shape((n, size, L...  2.65 us
    pallas_call x1, Pallas kernels, shards(): pl.pallas_call(adam_kernel, out_shape=[shape((n_rows, emb), F32)] * 3, gr...  2.51 us
  transfers between devices with their start and end apart: 1, of which 0 were waited for; matrix products, arithmetic and copies ran while one was open for 0% of the time, Pallas kernels for 73%

profile of v3, /device:TPU:0, one launch (start us, length us, event | category | flops | bytes accessed | tf_op | source)
XLA Modules:
  0.0 101.3 jit_solution(4979104449708207595)
XLA Ops:
  0.6 0.0 copy-start
  0.6 2.1 %place.1 = (s32[32,128]{1,0:T(8,128)}, s32[32,128]{1,0:T(8,128)}, s32[32,8]{1,0:T(8,128)}, s32[1,128]{1,0:T(1,128)}) custom-call(s32[16,128]{1,0:T(8,128)} %bitcast.17, s32[16,128]{1,0:T(8,128)} %bitcast.18, s32[1,128]{1,0:T(1,128)} %bitcast.13, s32[1,128]{1,0:T(1,128)} %bitcast.19, s32[1,128]{1,0:T(1,128)} %bitcast.20), custom_call_target="tpu_custom_call" | custom-call | tf_op jit(solution)/shard_map/place/pallas_call | solution.py:453
  2.8 0.8 add_bitcast_fusion
  3.5 0.1 copy.19
  3.6 14.5 %all_to_all.17 = s32[32,1,264]{2,1,0:T(1,128)S(1)} all-to-all(s32[32,1,264]{2,1,0:T(1,128)S(1)} %copy.19), channel_id=1, replica_groups=mesh['dp'=8,'mp'=4] {'dp','mp'}, dimensions={0} | all-to-all | bytes 67584 | tf_op jit(solution)/shard_map/all_to_all | solution.py:418
  18.1 0.1 reshape.43.wanted
  18.2 0.0 copy-start.2
  18.2 1.4 %copy-done.2 = bf16[1024,768]{1,0:T(8,128)(2,1)S(1)} copy-done((bf16[1024,768]{1,0:T(8,128)(2,1)S(1)}, bf16[1024,768]{1,0:T(8,128)(2,1)}, u32[]{:S(2)}) %copy-start.2) | copy-done | bytes 1572888
  19.6 1.4 %papers.2 = bf16[256,768]{1,0:T(8,128)(2,1)} custom-call(s32[2,128]{1,0:T(2,128)S(1)} %reshape.43.wanted, bf16[1024,768]{1,0:T(8,128)(2,1)S(1)} %copy-done.2), custom_call_target="tpu_custom_call" | custom-call | tf_op jit(solution)/shard_map/papers/pallas_call | solution.py:470
  21.0 0.0 copy-start.5
  21.0 0.0 copy-start.6
  21.0 0.0 copy-start.7
  21.0 2.7 %all-to-all-start.1 = ((bf16[32,8,768]{2,1,0:T(8,128)(2,1)}), bf16[32,8,768]{2,1,0:T(8,128)(2,1)S(1)}, u32[]{:S(2)}, u32[]{:S(2)}) async-start(bf16[32,8,768]{2,1,0:T(8,128)(2,1)} %bitcast.6), calls=%async_computation.1 | async-start | bytes 786432 | tf_op jit(solution)/shard_map/all_to_all | solution.py:418
  23.7 0.0 copy-done
  23.8 9.5 %fetch.1 = (f32[32,32,128]{2,1,0:T(8,128)S(1)}, f32[32,32,128]{2,1,0:T(8,128)S(1)}, f32[32,32,128]{2,1,0:T(8,128)S(1)}, f32[32,32,128]{2,1,0:T(8,128)S(1)}) custom-call(s32[32,128]{1,0:T(8,128)S(1)} %get-tuple-element.61.refs_0_.refs_7_, s32[32,128]{1,0:T(8,128)S(1)} %get-tuple-element.60.refs_1_.refs_8_, f32[2048,128]{1,0:T(8,128)S(1)} %copy-done), custom_call_target="tpu_custom_call" | custom-call | tf_op jit(solution)/shard_map/fetch/pallas_call | solution.py:481
  33.2 19.9 %sum_agg.1.refs_0_ = f32[128,128]{1,0:T(8,128)S(1)} custom-call(f32[32,32,128]{2,1,0:T(8,128)S(1)} %get-tuple-element.36.refs_0_, f32[32,32,128]{2,1,0:T(8,128)S(1)} %get-tuple-element.37.refs_1_, f32[32,32,128]{2,1,0:T(8,128)S(1)} %get-tuple-element.38.refs_2_, f32[32,32,128]{2,1,0:T(8,128)S(1)} %get-tuple-element.39.refs_3_), custom_call_target="tpu_custom_call" | custom-call | tf_op jit(solution)/shard_map/sum_agg/pallas_call | solution.py:495
  53.1 0.0 copy-done.5
  53.1 0.0 copy-done.6
  53.1 0.0 copy-done.7
  53.1 0.0 copy-done.8
  53.1 2.7 %layer.1 = (f32[32,48,128]{2,1,0:T(8,128)S(1)}, f32[32,48,128]{2,1,0:T(8,128)S(1)}, f32[32,48,128]{2,1,0:T(8,128)S(1)}, f32[32,48,128]{2,1,0:T(8,128)S(1)}, f32[...) custom-call(f32[128,128]{1,0:T(8,128)S(1)} %sum_agg.1.refs_0_, ...), custom_call_target="tpu_custom_call" | custom-call | tf_op jit(solution)/shard_map/layer/pallas_call | solution.py:508
  55.8 0.0 copy-start.3
  55.8 0.0 copy-start.4
  55.8 39.3 %exchange.1 = (f32[2048,256]{1,0:T(8,128)}, bf16[32,48,128]{2,1,0:T(8,128)(2,1)S(1)}, bf16[32,48,128]{2,1,0:T(8,128)(2,1)S(1)}, bf16[32,48,128]{2,1,0:T(8,128)(2...) custom-call(f32[32,48,128]{2,1,0:T(8,128)S(1)} %get-tuple-element.40.refs_0_, ...), custom_call_target="tpu_custom_call" | custom-call | tf_op jit(solution)/shard_map/exchange/pallas_call | solution.py:525
  95.2 0.0 copy-done.3
  95.2 0.0 copy-done.4
  95.2 0.0 copy-start.1
  95.2 1.6 %copy-done.1 = f32[2048,256]{1,0:T(8,128)S(1)} copy-done((f32[2048,256]{1,0:T(8,128)S(1)}, f32[2048,256]{1,0:T(8,128)}, u32[]{:S(2)}) %copy-start.1) | copy-done | bytes 2097176
  96.8 2.5 %adam.1 = (f32[2048,128]{1,0:T(8,128)}, f32[2048,128]{1,0:T(8,128)}, f32[2048,128]{1,0:T(8,128)}) custom-call(f32[2048,256]{1,0:T(8,128)S(1)} %copy-done.1, f32[2048,128]{1,0:T(8,128)S(1)} %copy-done, f32[2048,128]{1,0:T(8,128)S(1)} %copy-done.3, f32[2048,128]{1,0:T(8,128)S(1)} %copy-done.4), custom_call_target="tpu_custom_call" | custom-call | tf_op jit(solution)/shard_map/adam/pallas_call | solution.py:537
  99.3 0.0 all-to-all-done.1
  99.3 0.0 copy-done.9
  99.3 2.0 %unpack.1 = (f32[768,1024]{1,0:T(8,128)}, f32[128,1024]{1,0:T(8,128)}, bf16[128,768]{1,0:T(8,128)(2,1)}) custom-call(bf16[32,48,128]{2,1,0:T(8,128)(2,1)S(1)} %get-tuple-element.51.refs_0_, bf16[32,48,128]{2,1,0:T(8,128)(2,1)S(1)} %get-tuple-element.52.refs_1_, bf16[32,48,128]{2,1,0:T(8,128)(2,1)S(1)} %get-tuple-element.53.refs_2_, ...), custom_call_target="tpu_custom_call" | custom-call | tf_op jit(solution)/shard_map/unpack/pallas_call | solution.py:547
  (5 shorter events, 0.0 us)
Async XLA Ops:
  0.6 23.1 %copy-start = (f32[2048,128]{1,0:T(8,128)S(1)}, f32[2048,128]{1,0:T(8,128)}, u32[]{:S(2)}) copy-start(f32[2048,128]{1,0:T(8,128)} %table.1) | copy-start | bytes 3145732
  18.2 1.4 %copy-start.2 = (bf16[1024,768]{1,0:T(8,128)(2,1)S(1)}, bf16[1024,768]{1,0:T(8,128)(2,1)}, u32[]{:S(2)}) copy-start(bf16[1024,768]{1,0:T(8,128)(2,1)} %papers.3) | copy-start | bytes 4718596
  21.0 32.1 %copy-start.5 = (f32[128,1024]{1,0:T(8,128)S(1)}, f32[128,1024]{1,0:T(8,128)}, u32[]{:S(2)}) copy-start(f32[128,1024]{1,0:T(8,128)} %refs_5_.1) | copy-start | bytes 1572868
  21.0 32.1 %copy-start.6 = (bf16[128,1024]{1,0:T(8,128)(2,1)S(1)}, bf16[128,1024]{1,0:T(8,128)(2,1)}, u32[]{:S(2)}) copy-start(bf16[128,1024]{1,0:T(8,128)(2,1)} %refs_4_.1) | copy-start | bytes 786436
  21.0 32.1 %copy-start.7 = (bf16[128,768]{1,0:T(8,128)(2,1)S(1)}, bf16[128,768]{1,0:T(8,128)(2,1)}, u32[]{:S(2)}) copy-start(bf16[128,768]{1,0:T(8,128)(2,1)} %refs_2_.3) | copy-start | bytes 589828
  21.0 32.2 %copy-start.8 = (s32[128]{0:T(128)S(1)}, s32[128]{0:T(128)}, u32[]{:S(2)}) copy-start(s32[128]{0:T(128)} %param.16) | copy-start | bytes 1540
  21.0 78.3 %all-to-all-start.1 = ((bf16[32,8,768]{2,1,0:T(8,128)(2,1)}), bf16[32,8,768]{2,1,0:T(8,128)(2,1)S(1)}, u32[]{:S(2)}, u32[]{:S(2)}) async-start(bf16[32,8,768]{2,1,0:T(8,128)(2,1)} %bitcast.6), calls=%async_computation.1 | async-start | bytes 786432 | tf_op jit(solution)/shard_map/all_to_all | solution.py:418
  55.8 39.4 %copy-start.3 = (f32[2048,128]{1,0:T(8,128)S(1)}, f32[2048,128]{1,0:T(8,128)}, u32[]{:S(2)}) copy-start(f32[2048,128]{1,0:T(8,128)} %m1.1) | copy-start | bytes 3145732
  55.8 39.4 %copy-start.4 = (f32[2048,128]{1,0:T(8,128)S(1)}, f32[2048,128]{1,0:T(8,128)}, u32[]{:S(2)}) copy-start(f32[2048,128]{1,0:T(8,128)} %m2.1) | copy-start | bytes 3145732
  95.2 1.6 %copy-start.1 = (f32[2048,256]{1,0:T(8,128)S(1)}, f32[2048,256]{1,0:T(8,128)}, u32[]{:S(2)}) copy-start(f32[2048,256]{1,0:T(8,128)} %get-tuple-element.47.got) | copy-start | bytes 6291460
  96.8 2.5 %copy-start.9 = (s32[1,128]{1,0:T(1,128)S(1)}, s32[1,128]{1,0:T(1,128)}, u32[]{:S(2)}) copy-start(s32[1,128]{1,0:T(1,128)} %get-tuple-element.56.refs_5_) | copy-start | bytes 1540
